TPU v7x, 256 devices: a whole 4x4x8 slice. The times are simulated.
256 devices in a mesh: dp: 32 (over y, z), tensor: 8 (over x, core).
Axes of the slice: x: 4, y: 4, z: 8, core: 2. Of those that a mesh axis runs over, the one named last changes fastest.
Arguments:
- attn_in: bfloat16 [64, 1024, 4096], P('dp', None, 'tensor'), may hold values from -6 to 6
- v_grad: bfloat16 [64, 1024, 1024], P('dp', None, 'tensor'), may hold values from -6 to 6
- mlp_hidden: bfloat16 [64, 1024, 14336], P('dp', None, 'tensor'), may hold values from -6 to 6
- out_grad: bfloat16 [64, 1024, 4096], P('dp', None, 'tensor'), may hold values from -6 to 6
- proj_in_attn: bfloat16 [64, 4096], P(None, 'tensor'), may hold values from -0.09375 to 0.09375
- proj_out_value: bfloat16 [64, 1024], P(None, 'tensor'), may hold values from -0.1875 to 0.1875
- proj_in_mlp: bfloat16 [64, 14336], P(None, 'tensor'), may hold values from -0.046875 to 0.046875
- proj_out_mlp: bfloat16 [64, 4096], P(None, 'tensor'), may hold values from -0.09375 to 0.09375
- query_features: bfloat16 [2, 1024, 4096], P(None, 'tensor', 'dp'), may hold values from -0.0625 to 0.0625
Outputs:
- fisher: float32 [4096, 2, 4096], P('dp', None, 'tensor')
- scores: float32 [64, 1024], P('dp', 'tensor')
All inputs are finite; a program needn't handle non-finite values.
Results may differ from a plain program's by a relative error of at most 0.0055.
The roundings to bfloat16 on the way count: a program that leaves them out, or rounds other values in their place, can miss the bound.
Values may be sent and summed in bfloat16 or wider, within the bound.
No kernel may reach another device: no remote copies, remote signals or barrier semaphores. Data moves between devices by JAX's collectives and lax.ppermute only.
A program may use at most 128 MiB of HBM per device.

v0:
```python
import math

import jax
import jax.numpy as jnp
from jax import lax
from jax.sharding import PartitionSpec as P


def project_side(activations, projection):
    return jnp.einsum("esd,kd->esk", activations, projection, preferred_element_type=jnp.float32)


def outer_products(projected, low_rank):
    rounded = projected.astype(jnp.bfloat16)
    value_part = jnp.einsum(
        "esa,esb->eab",
        rounded[:, :, 0:low_rank],
        rounded[:, :, low_rank : 2 * low_rank],
        preferred_element_type=jnp.float32,
    )
    down_part = jnp.einsum(
        "esa,esb->eab",
        rounded[:, :, 2 * low_rank : 3 * low_rank],
        rounded[:, :, 3 * low_rank : 4 * low_rank],
        preferred_element_type=jnp.float32,
    )
    sequences = projected.shape[0]
    return jnp.stack(
        [
            value_part.reshape(sequences, low_rank * low_rank),
            down_part.reshape(sequences, low_rank * low_rank),
        ],
        axis=1,
    )


def shards(
    attn_in,
    v_grad,
    mlp_hidden,
    out_grad,
    proj_in_attn,
    proj_out_value,
    proj_in_mlp,
    proj_out_mlp,
    query_features,
):
    low_rank = proj_in_attn.shape[0]
    length = attn_in.shape[1]
    partial_proj = jnp.concatenate(
        [
            project_side(v_grad, proj_out_value),
            project_side(attn_in, proj_in_attn),
            project_side(out_grad, proj_out_mlp),
            project_side(mlp_hidden, proj_in_mlp),
        ],
        axis=2,
    )
    summed = lax.psum(partial_proj, "tensor")
    raw_sums = outer_products(summed, low_rank)
    features = (raw_sums * (1.0 / math.sqrt(length))).astype(jnp.bfloat16)
    sequences = features.shape[0]
    feat_total = features.shape[2]
    dp_count = lax.axis_size("dp")
    row_count = feat_total // dp_count
    col_count = feat_total // lax.axis_size("tensor")
    total_examples = sequences * dp_count
    dp_pos = lax.axis_index("dp")
    tp_pos = lax.axis_index("tensor")
    widened = features.astype(jnp.float32)
    local_squares = jnp.sum(widened * widened, axis=(0, 2))
    my_columns = lax.dynamic_slice_in_dim(features, tp_pos * col_count, col_count, 2)
    gram_block = lax.psum_scatter(
        jnp.einsum("epf,epc->fpc", features, my_columns, preferred_element_type=jnp.float32),
        "dp",
        scatter_dimension=0,
        tiled=True,
    )
    squares = lax.psum(local_squares, "dp")
    damping = 0.5 * squares / (total_examples * feat_total)
    row_global = dp_pos * row_count + jnp.arange(row_count, dtype=jnp.int32)
    col_global = tp_pos * col_count + jnp.arange(col_count, dtype=jnp.int32)
    identity_mask = (row_global[:, None, None] == col_global[None, None, :]).astype(jnp.float32)
    fisher = gram_block / total_examples + damping[None, :, None] * identity_mask
    norm_scale = jnp.sqrt(jnp.mean(widened * widened, axis=(1, 2)) + 1e-06)
    partial_scores = jnp.einsum(
        "epf,pqf->eq",
        features,
        lax.all_gather(query_features, "dp", axis=2, tiled=True),
        preferred_element_type=jnp.float32,
    )
    scores = partial_scores / norm_scale[:, None]
    return (fisher, scores)


def solution(mesh):
    return jax.shard_map(
        shards,
        mesh=mesh,
        in_specs=(
            P("dp", None, "tensor"),
            P("dp", None, "tensor"),
            P("dp", None, "tensor"),
            P("dp", None, "tensor"),
            P(None, "tensor"),
            P(None, "tensor"),
            P(None, "tensor"),
            P(None, "tensor"),
            P(None, "tensor", "dp"),
        ),
        out_specs=(P("dp", None, "tensor"), P("dp", "tensor")),
        check_vma=False,
    )
```

profile of v0, /device:TPU:32, one launch (start us, length us, event | category | flops | bytes accessed | tf_op | source)
XLA Modules:
  0.0 345.9 jit_solution(12313306243608434948)
XLA Ops:
  7.2 0.0 copy-start
  7.2 0.0 copy-start.5
  7.2 0.0 all-gather.2.cloned.1.call-start
  7.2 0.7 all-gather.2.cloned.1.call-update
  7.9 0.0 copy-start.6
  7.9 0.0 reduce-scatter.2.cloned.1.call-start
  8.0 0.8 copy-done
  8.8 0.0 copy-start.1
  8.8 0.0 copy-start.3
  8.8 1.7 fusion.10
  10.5 0.0 copy-done.5
  10.5 0.0 copy-done.1
  10.5 0.0 copy-start.4
  10.5 1.5 fusion.12
  12.1 0.0 copy-done.6
  12.1 0.0 copy-done.3
  12.1 0.3 fusion.16
  12.4 0.0 copy-done.4
  12.4 0.0 copy-start.2
  12.4 5.4 %fusion.7 = f32[2,1024,64]{1,2,0:T(8,128)S(1)} fusion(bf16[2,1024,1792]{2,1,0:T(8,128)(2,1)} %param.11, bf16[64,1792]{1,0:T(8,128)(2,1)S(1)} %copy-done.4), kind=kOutput, calls=%fused_computation.12 | convolution fusion | flops 469762048 | bytes 8093696 | tf_op jit(solution)/shard_map/esd,kd->esk/dot_general | solution.py:10
  17.9 0.0 copy-done.2
  17.9 1.6 pad_maximum_fusion
  19.4 55.3 %all-reduce.1 = bf16[2,1024,256]{1,2,0:T(8,128)(2,1)S(1)} all-reduce(f32[2,1024,256]{1,2,0:T(8,128)} %pad_maximum_fusion), channel_id=1, replica_groups=mesh['dp'=32,'tensor'=8] {'tensor'}, use_global_device_ids=true, to_apply=%region_0.0 | all-reduce | flops 524288 | bytes 3145728 | tf_op jit(solution)/shard_map/psum | solution.py:59
  74.7 0.2 fusion.4
  74.9 0.1 stack_reshape.6
  75.0 0.2 fusion.1
  75.2 0.1 stack_reshape.7
  75.3 0.2 fusion.14
  75.6 8.1 %convolution_bitcast_fusion = f32[4096,2,512]{0,2,1:T(8,128)} fusion(bf16[2,2,4096]{2,0,1:T(2,128)(2,1)S(1)} %get-tuple-element.6, s32[]{:T(128)S(6)} %select_n.3), kind=kOutput, calls=%fused_computation | convolution fusion | flops 16777216 | bytes 16814084 | tf_op jit(solution)/shard_map/epf,epc->fpc/dot_general | solution.py:74
  83.7 0.0 reduce-scatter.2.cloned.1.call-update
  83.7 74.3 %psum.15 = f32[2]{0:T(128)S(1)} all-reduce(f32[2]{0:T(128)S(1)} %get-tuple-element.5), channel_id=1, replica_groups=mesh['dp'=32,'tensor'=8] {'dp'}, use_global_device_ids=true, to_apply=%region_3.0 | all-reduce | flops 2 | bytes 16 | tf_op jit(solution)/shard_map/psum | solution.py:79
  158.0 0.1 compare_convert_fusion
  158.2 0.0 all-gather.2.cloned.1.call-done
  158.2 2.9 fusion
  161.1 175.8 %reduce-scatter.2.cloned.1.call-done = f32[128,2,512]{0,2,1:T(8,128)} async-done(((f32[4096,2,512]{0,2,1:T(8,128)}), f32[128,2,512]{0,2,1:T(8,128)}) %reduce-scatter.2.cloned.1.call-update) | async-done | bytes 524304 | tf_op jit(solution)/shard_map/reduce_scatter | solution.py:73
  336.9 1.2 multiply_add_fusion
  338.1 1.0 copy.11
  (4 shorter events, 0.0 us)
Async XLA Ops:
  7.2 1.6 copy-start
  7.2 3.3 copy-start.5
  7.2 151.0 %all-gather.2.cloned.1.call-start = ((), (), s32[]{:S(2)}) async-start(), calls=%async_computation.2 | async-start | bytes 2162688 | tf_op jit(solution)/shard_map/all_gather | solution.py:89
  7.9 4.2 %copy-start.6 = (bf16[64,128]{1,0:T(8,128)(2,1)S(1)}, bf16[64,128]{1,0:T(8,128)(2,1)}, u32[]{:S(2)}) copy-start(bf16[64,128]{1,0:T(8,128)(2,1)} %param.14) | copy-start | bytes 49156
  7.9 329.0 %reduce-scatter.2.cloned.1.call-start = ((), (), s32[]{:S(2)}) async-start(), calls=%async_computation.1 | async-start | bytes 17301504 | tf_op jit(solution)/shard_map/reduce_scatter | solution.py:73
  8.8 1.7 copy-start.1
  8.8 3.3 copy-start.3
  10.5 1.9 copy-start.4
  12.4 5.5 %copy-start.2 = (f32[2,1024,64]{1,2,0:T(8,128)S(1)}, f32[2,1024,64]{1,2,0:T(8,128)}, u32[]{:S(2)}) copy-start(f32[2,1024,64]{1,2,0:T(8,128)} %fusion.12) | copy-start | bytes 1572868
Sparse Core Ops, SparseCore 0:
  10.5 77.4 all-gather.1
  92.1 244.7 reduce-scatter.1
where the time goes:
time: 347 us; the launch traced here: 346 us
  waiting for transfers between devices  177 us (51%)
  blocking collectives  130 us (37%)
  matrix products  20.4 us (6%)
  between operations  14.2 us (4%)
    reduce_scatter x1, waiting for transfers between devices, shards(): lax.psum_scatter(jnp.einsum('epf,epc->fpc', features, my_columns, preferr...  176 us
    psum x1, blocking collectives, shards(): squares = lax.psum(local_squares, 'dp')  74.3 us
    psum x1, blocking collectives, shards(): summed = lax.psum(partial_proj, 'tensor')  55.3 us
    dot_general x4, matrix products, project_side(): jnp.einsum('esd,kd->esk', activations, projection, preferred_element_type...  9.01 us
    dot_general x1, matrix products, shards(): jnp.einsum('epf,epc->fpc', features, my_columns, preferred_element_type=j...  8.11 us
  transfers between devices with their start and end apart: 2, of which 1 were waited for; matrix products, arithmetic and copies ran while one was open for 7% of the time, Pallas kernels for 0%

commit v1 on v0

v1 whole, which is shorter than its diff:
```python
import functools
import math

import jax
import jax.numpy as jnp
from jax import lax
from jax.experimental import pallas as pl
from jax.experimental.pallas import tpu as pltpu
from jax.sharding import PartitionSpec as P

F32 = jnp.float32
BF16 = jnp.bfloat16
LANES = 128
VMEM = pltpu.VMEM
NT = (((1,), (1,)), ((), ()))
TN = (((0,), (0,)), ((), ()))


def dot(a, b, dims):
    return lax.dot_general(a, b, dims, preferred_element_type=F32)


def project_kernel(place, v_ref, a_ref, g_ref, m_ref, wv_ref, wa_ref, wg_ref, wm_ref, out_ref):
    sequence, block = pl.program_id(0), pl.program_id(1)
    tokens = v_ref.shape[1]
    rank = wv_ref.shape[0]
    rows = pl.ds(pl.multiple_of(block * tokens, tokens), tokens)
    first = lax.rem(2 * sequence + 4 - place[0], 4)
    second = lax.rem(2 * sequence + 5 - place[0], 4)
    out_ref[first, rows, 0:rank] = dot(v_ref[0], wv_ref[...], NT)
    out_ref[first, rows, rank:LANES] = dot(a_ref[0], wa_ref[...], NT)
    out_ref[second, rows, 0:rank] = dot(g_ref[0], wg_ref[...], NT)
    out_ref[second, rows, rank:LANES] = dot(m_ref[0], wm_ref[...], NT)


def project(place, acts, weights, tokens):
    sequences, length, _ = acts[0].shape
    half = length // 2
    blocks = half // tokens
    act_specs = [pl.BlockSpec((1, tokens, a.shape[2]), lambda e, b, s: (e, s[1] * blocks + b, 0)) for a in acts]
    weight_specs = [pl.BlockSpec(w.shape, lambda e, b, s: (0, 0)) for w in weights]
    flops = 2 * sequences * half * sum(w.size for w in weights)
    return pl.pallas_call(
        project_kernel,
        grid_spec=pltpu.PrefetchScalarGridSpec(
            num_scalar_prefetch=1,
            grid=(sequences, blocks),
            in_specs=act_specs + weight_specs,
            out_specs=pl.BlockSpec((4, half, LANES), lambda e, b, s: (0, 0, 0)),
        ),
        out_shape=jax.ShapeDtypeStruct((4, half, LANES), F32),
        cost_estimate=pl.CostEstimate(flops=flops, bytes_accessed=sum(a.size for a in acts) + 4 * half * LANES * 4, transcendentals=0),
        compiler_params=pltpu.CompilerParams(vmem_limit_bytes=58 * 2**20),
        name="project",
    )(place, *acts, *weights)


def add_kernel(own_ref, other_ref, *out_refs):
    for slot, out_ref in enumerate(out_refs):
        out_ref[...] = own_ref[slot] + other_ref[slot]


def add_cores(own, other):
    shape = jax.ShapeDtypeStruct(own.shape[1:], F32)
    return pl.pallas_call(
        add_kernel,
        out_shape=[shape] * 4,
        in_specs=[pl.BlockSpec(memory_space=VMEM)] * 2,
        out_specs=[pl.BlockSpec(memory_space=VMEM)] * 4,
        cost_estimate=pl.CostEstimate(flops=own.size, bytes_accessed=12 * own.size, transcendentals=0),
        compiler_params=pltpu.CompilerParams(vmem_limit_bytes=8 * 2**20),
        name="add_cores",
    )(own, other)


def outer_kernel(rank, a_ref, b_ref, c_ref, d_ref, out_ref, held):
    vectors = ((a_ref[...] + b_ref[...]) + (c_ref[...] + d_ref[...])).astype(BF16)
    held[...] = dot(vectors[:, 0:rank], vectors, TN)
    even = held[pl.ds(0, rank // 2, stride=2), :]
    odd = held[pl.ds(1, rank // 2, stride=2), :]
    lane = lax.broadcasted_iota(jnp.int32, even.shape, 1)
    rows = jnp.where(lane < rank, pltpu.roll(even, rank, 1), odd)
    for target in range(out_ref.shape[0]):
        out_ref[target] = rows


def outer(parts, rank, width):
    return pl.pallas_call(
        functools.partial(outer_kernel, rank),
        out_shape=jax.ShapeDtypeStruct((width, rank // 2, LANES), F32),
        in_specs=[pl.BlockSpec(memory_space=VMEM)] * 4,
        out_specs=pl.BlockSpec(memory_space=VMEM),
        scratch_shapes=[pltpu.VMEM((rank, LANES), F32)],
        compiler_params=pltpu.CompilerParams(vmem_limit_bytes=8 * 2**20),
        name="outer",
    )(*parts)


def features_kernel(scale, place, sums_ref, send_ref, norm_ref):
    blocks = send_ref.shape[0]
    feats = {}
    squares = {}
    for e in range(2):
        for p in range(2):
            chip = 2 * e + p
            rounded = ((sums_ref[2 * chip] + sums_ref[2 * chip + 1]) * scale).astype(BF16)
            wide = rounded.astype(F32)
            feats[e, p] = wide
            squares[e, p] = jnp.sum(jnp.sum(wide * wide, axis=1, keepdims=True), axis=0, keepdims=True)
    for e in range(2):
        mean = (squares[e, 0] + squares[e, 1]) / (2.0 * blocks * LANES)
        norm_ref[e : e + 1, :] = jnp.broadcast_to(jnp.sqrt(mean + 1e-06), (1, LANES))
    row = lax.broadcasted_iota(jnp.int32, (16, LANES), 0)
    for p in range(2):
        total = squares[0, p] + squares[1, p]
        high = total.astype(BF16).astype(F32)
        middle = (total - high).astype(BF16).astype(F32)
        low = total - high - middle
        base = jnp.zeros((16, LANES), F32)
        for e in range(2):
            for k in range(4):
                at = place[1] * 4 + k
                base = jnp.where(row == 5 * e + 1 + k, rounded_row(sums_ref, scale, 2 * e + p, at), base)
        for k, term in enumerate((high, middle, low)):
            base = jnp.where(row == 10 + k, term, base)
        for i in range(blocks):
            tile = jnp.where(row == 0, feats[0, p][i : i + 1, :], base)
            tile = jnp.where(row == 5, feats[1, p][i : i + 1, :], tile)
            send_ref[i, p] = tile.astype(BF16)


def rounded_row(sums_ref, scale, chip, at):
    summed = sums_ref[2 * chip, pl.ds(at, 1), :] + sums_ref[2 * chip + 1, pl.ds(at, 1), :]
    return (summed * scale).astype(BF16).astype(F32)


def features(place, sums, scale, dp):
    blocks = sums.shape[1]
    return pl.pallas_call(
        functools.partial(features_kernel, scale),
        out_shape=[
            jax.ShapeDtypeStruct((dp, 2, 16, LANES), BF16),
            jax.ShapeDtypeStruct((2, LANES), F32),
        ],
        in_specs=[pl.BlockSpec(memory_space=pltpu.SMEM), pl.BlockSpec(memory_space=VMEM)],
        out_specs=[pl.BlockSpec(memory_space=VMEM)] * 2,
        compiler_params=pltpu.CompilerParams(vmem_limit_bytes=8 * 2**20),
        name="features",
    )(place, sums)


def fisher_kernel(examples, place, got_ref, out_ref, held):
    sources = got_ref.shape[0]
    count = examples * 32 * LANES
    row = lax.broadcasted_iota(jnp.int32, (LANES, LANES), 0)
    lane = lax.broadcasted_iota(jnp.int32, (LANES, LANES), 1)
    for p in range(2):
        held[...] = got_ref[:, p].astype(F32).reshape(sources * 16, LANES)

        def pick(r):
            return held[pl.ds(r, sources, stride=16), :]

        mine = jnp.concatenate([pick(0), pick(5)], axis=0).astype(BF16)
        total = jnp.sum(pick(10) + pick(11) + pick(12), axis=0, keepdims=True)
        damping = 0.5 * total / count
        for k in range(4):
            theirs = jnp.concatenate([pick(1 + k), pick(6 + k)], axis=0).astype(BF16)
            block = dot(mine, theirs, TN) * (1.0 / examples)
            on = jnp.logical_and(row == lane, place[0] - 4 * place[1] == k)
            out_ref[:, p, k * LANES : (k + 1) * LANES] = block + jnp.where(on, damping, 0.0)


def fisher_block(place, got, examples):
    return pl.pallas_call(
        functools.partial(fisher_kernel, examples),
        out_shape=jax.ShapeDtypeStruct((LANES, 2, 4 * LANES), F32),
        in_specs=[pl.BlockSpec(memory_space=pltpu.SMEM), pl.BlockSpec(memory_space=VMEM)],
        out_specs=pl.BlockSpec(memory_space=VMEM),
        scratch_shapes=[pltpu.VMEM((got.shape[0] * 16, LANES), F32)],
        compiler_params=pltpu.CompilerParams(vmem_limit_bytes=8 * 2**20),
        name="fisher",
    )(place, got)


def scores_kernel(got_ref, query_ref, out_ref, held):
    sources = got_ref.shape[0]
    total = None
    for p in range(2):
        held[...] = got_ref[:, p].astype(F32).reshape(sources * 16, LANES)
        pair = [held[pl.ds(5 * e, sources, stride=16), :] for e in range(2)]
        part = dot(jnp.concatenate(pair, axis=0).astype(BF16), query_ref[p], NT)
        total = part if total is None else total + part
    out_ref[:, 0, :] = total[0:sources]
    out_ref[:, 1, :] = total[sources:]


def score_shares(got, query):
    sources = got.shape[0]
    return pl.pallas_call(
        scores_kernel,
        out_shape=jax.ShapeDtypeStruct((sources, 2, query.shape[1]), F32),
        in_specs=[pl.BlockSpec(memory_space=VMEM)] * 2,
        out_specs=pl.BlockSpec(memory_space=VMEM),
        scratch_shapes=[pltpu.VMEM((sources * 16, LANES), F32)],
        compiler_params=pltpu.CompilerParams(vmem_limit_bytes=8 * 2**20),
        name="score_shares",
    )(got, query)


def shards(
    attn_in,
    v_grad,
    mlp_hidden,
    out_grad,
    proj_in_attn,
    proj_out_value,
    proj_in_mlp,
    proj_out_mlp,
    query_features,
):
    rank = proj_in_attn.shape[0]
    length = attn_in.shape[1]
    dp = lax.axis_size("dp")
    width = lax.axis_size("tensor")
    examples = attn_in.shape[0] * dp
    dp_pos = lax.axis_index("dp")
    tp_pos = lax.axis_index("tensor")
    chip, core = tp_pos // 2, tp_pos % 2

    acts = (v_grad, attn_in, out_grad, mlp_hidden)
    weights = (proj_out_value, proj_in_attn, proj_out_mlp, proj_in_mlp)
    theirs = project(jnp.stack([chip, 1 - core]).astype(jnp.int32), acts, weights, 256)
    other = lax.ppermute(theirs, "tensor", [(k, k ^ 1) for k in range(width)])
    own = project(jnp.stack([chip, core]).astype(jnp.int32), acts, weights, 256)
    kept, *sent = add_cores(own, other)
    parts = [kept] + [
        lax.ppermute(sent[s - 1], "tensor", [(k, (k + 2 * s) % width) for k in range(width)]) for s in (1, 2, 3)
    ]
    partial = outer(parts, rank, width)
    sums = lax.all_to_all(partial, "tensor", 0, 0, tiled=True)
    place = jnp.stack([dp_pos, tp_pos]).astype(jnp.int32)
    send, norms = features(place, sums, 1.0 / math.sqrt(length), dp)
    got = lax.all_to_all(send, "dp", 0, 0, tiled=True)
    shares = lax.all_to_all(score_shares(got, query_features), "dp", 0, 0, tiled=True)
    fisher = fisher_block(place, got, examples)
    scores = jnp.sum(shares, axis=0) / norms[:, 0:1]
    return (fisher, scores)


def solution(mesh):
    return jax.shard_map(
        shards,
        mesh=mesh,
        in_specs=(
            P("dp", None, "tensor"),
            P("dp", None, "tensor"),
            P("dp", None, "tensor"),
            P("dp", None, "tensor"),
            P(None, "tensor"),
            P(None, "tensor"),
            P(None, "tensor"),
            P(None, "tensor"),
            P(None, "tensor", "dp"),
        ),
        out_specs=(P("dp", None, "tensor"), P("dp", "tensor")),
        check_vma=False,
    )
```

time: 347 us -> 83.7 us (0.24)
  waiting for transfers between devices: 177 us -> 23.7 us
  blocking collectives: 130 us -> 23.2 us
  matrix products: 20.4 us -> 0 us
  Pallas kernels: 0 us -> 17.7 us
  starting transfers between devices: 0.08 us -> 14.2 us
  between operations: 14.2 us -> 0.69 us
    reduce_scatter x1 -> x0, waiting for transfers between devices: 176 us -> none  [shards(): lax.psum_scatter(jnp.einsum('epf,epc->fpc', features, my_columns, preferr...]
    psum x2 -> x0, blocking collectives: 130 us -> none  [the longest x1 74.3 us: shards(): squares = lax.psum(local_squares, 'dp')]
    all_to_all x0 -> x1, blocking collectives: none -> 23.2 us  [shards(): got = lax.all_to_all(send, 'dp', 0, 0, tiled=True)]
    dot_general x8 -> x0, matrix products: 20.4 us -> none  [the longest x4 9.01 us: project_side(): jnp.einsum('esd,kd->esk', activations, projection, preferred_element_type...]
    pallas_call x0 -> x7, Pallas kernels: none -> 17.7 us  [the longest x2 13.3 us: project(): pl.pallas_call(project_kernel, grid_spec=pltpu.PrefetchScalarGridSpec(num...]
    all_to_all x0 -> x2, waiting for transfers between devices: none -> 12.9 us  [the longest x1 6.79 us: shards(): lax.all_to_all(score_shares(got, query_features), 'dp', 0, 0, tiled=True)]
    ppermute x0 -> x4, waiting for transfers between devices: none -> 10.9 us  [the longest x3 10.9 us: shards(): lax.ppermute(sent[s - 1], 'tensor', [(k, (k + 2 * s) % width) for k in ra...]
    all_to_all x0 -> x2, starting transfers between devices: none -> 8.5 us  [the longest x1 4.56 us: shards(): lax.all_to_all(score_shares(got, query_features), 'dp', 0, 0, tiled=True)]
  transfers between devices with their start and end apart: 2 -> 6, of which waited for: 1 -> 4; matrix products, arithmetic and copies ran while one was open for 7% -> 1% of each run, Pallas kernels for 0% -> 10%
where the time goes in v1:
time: 83.7 us; the launch traced here: 83 us
  waiting for transfers between devices  23.7 us (28%)
  blocking collectives  23.2 us (28%)
  Pallas kernels  17.7 us (21%)
  starting transfers between devices  14.2 us (17%)
  other arithmetic  2.06 us (2%)
  local copies, waits for them, and re-layouts  1.34 us (2%)
    all_to_all x1, blocking collectives, shards(): got = lax.all_to_all(send, 'dp', 0, 0, tiled=True)  23.2 us
    pallas_call x2, Pallas kernels, project(): pl.pallas_call(project_kernel, grid_spec=pltpu.PrefetchScalarGridSpec(num...  13.3 us
    ppermute x3, waiting for transfers between devices, shards(): lax.ppermute(sent[s - 1], 'tensor', [(k, (k + 2 * s) % width) for k in ra...  10.9 us
    all_to_all x1, waiting for transfers between devices, shards(): lax.all_to_all(score_shares(got, query_features), 'dp', 0, 0, tiled=True)  6.79 us
    all_to_all x1, waiting for transfers between devices, shards(): sums = lax.all_to_all(partial, 'tensor', 0, 0, tiled=True)  6.06 us
    ppermute x3, starting transfers between devices, shards(): lax.ppermute(sent[s - 1], 'tensor', [(k, (k + 2 * s) % width) for k in ra...  5.74 us
    all_to_all x1, starting transfers between devices, shards(): lax.all_to_all(score_shares(got, query_features), 'dp', 0, 0, tiled=True)  4.56 us
    all_to_all x1, starting transfers between devices, shards(): sums = lax.all_to_all(partial, 'tensor', 0, 0, tiled=True)  3.94 us
  transfers between devices with their start and end apart: 6, of which 4 were waited for; matrix products, arithmetic and copies ran while one was open for 1% of the time, Pallas kernels for 10%

profile of v1, /device:TPU:32, one launch (start us, length us, event | category | flops | bytes accessed | tf_op | source)
XLA Modules:
  0.0 83.0 jit_solution(6910967213086928388)
XLA Ops:
  0.7 0.6 pad_add_fusion.2.place
  1.3 6.6 %project.3 = f32[4,512,128]{2,1,0:T(8,128)} custom-call(s32[2]{0:T(128)} %pad_add_fusion.2.place, bf16[2,1024,128]{2,1,0:T(8,128)(2,1)} %v_ref.3, bf16[2,1024,512]{2,1,0:T(8,128)(2,1)} %a_ref.3, bf16[2,1024,512]{2,1,0:T(8,128)(2,1)} %g_ref.3, bf16[2,1024,1792]{2,1,0:T(8,128)(2,1)} %m_ref.3, bf16[64,128]{1,0:T(8,128)(2,1)} %wv_ref.3, bf16[64,512]{1,0:T(8,128)(2,1)} %wa_ref.3, ...), custom_call_target="tpu_custom_call" | custom-call | flops 385875968 | bytes 7077888 | tf_op jit(solution)/shard_map/project/pallas_call | solution.py:43
  7.9 0.0 collective-permute-start
  7.9 0.7 pad_add_fusion.1.place
  8.6 6.7 %project.2.own_ref = f32[4,512,128]{2,1,0:T(8,128)} custom-call(s32[2]{0:T(128)} %pad_add_fusion.1.place, bf16[2,1024,128]{2,1,0:T(8,128)(2,1)} %v_ref.3, bf16[2,1024,512]{2,1,0:T(8,128)(2,1)} %a_ref.3, bf16[2,1024,512]{2,1,0:T(8,128)(2,1)} %g_ref.3, bf16[2,1024,1792]{2,1,0:T(8,128)(2,1)} %m_ref.3, bf16[64,128]{1,0:T(8,128)(2,1)} %wv_ref.3, ...), custom_call_target="tpu_custom_call" | custom-call | flops 385875968 | bytes 7077888 | tf_op jit(solution)/shard_map/project/pallas_call | solution.py:43
  15.2 0.0 collective-permute-done.other_ref
  15.2 0.0 copy-start
  15.2 1.2 %copy-done = f32[4,512,128]{2,1,0:T(8,128)S(1)} copy-done((f32[4,512,128]{2,1,0:T(8,128)S(1)}, f32[4,512,128]{2,1,0:T(8,128)}, u32[]{:S(2)}) %copy-start) | copy-done | bytes 1048600
  16.4 0.0 copy-start.1
  16.4 0.1 add_cores.1
  16.6 1.6 %collective-permute-start.1 = (f32[512,128]{1,0:T(8,128)S(1)}, f32[512,128]{1,0:T(8,128)S(1)}, u32[]{:S(2)}, u32[]{:S(2)}) collective-permute-start(f32[512,128]{1,0:T(8,128)S(1)} %get-tuple-element.9), channel_id=1, source_target_pairs={{0,2},{1,3},{2,4},{3,5},{4,6},{5,7},{6,0},{7,1},{8,10},{9,11},{10,... | collective-permute-start | bytes 786440 | tf_op jit(solution)/shard_map/ppermute | solution.py:237
  18.1 2.7 %collective-permute-start.2 = (f32[512,128]{1,0:T(8,128)S(1)}, f32[512,128]{1,0:T(8,128)S(1)}, u32[]{:S(2)}, u32[]{:S(2)}) collective-permute-start(f32[512,128]{1,0:T(8,128)S(1)} %get-tuple-element.10), channel_id=1, source_target_pairs={{0,4},{1,5},{2,6},{3,7},{4,0},{5,1},{6,2},{7,3},{8,12},{9,13},{10,... | collective-permute-start | bytes 786440 | tf_op jit(solution)/shard_map/ppermute | solution.py:237
  20.9 1.4 %collective-permute-start.3 = (f32[512,128]{1,0:T(8,128)S(1)}, f32[512,128]{1,0:T(8,128)S(1)}, u32[]{:S(2)}, u32[]{:S(2)}) collective-permute-start(f32[512,128]{1,0:T(8,128)S(1)} %get-tuple-element.11), channel_id=1, source_target_pairs={{0,6},{1,7},{2,0},{3,1},{4,2},{5,3},{6,4},{7,5},{8,14},{9,15},{10,... | collective-permute-start | bytes 786440 | tf_op jit(solution)/shard_map/ppermute | solution.py:237
  22.3 4.3 %collective-permute-done.1.b_ref = f32[512,128]{1,0:T(8,128)S(1)} collective-permute-done((f32[512,128]{1,0:T(8,128)S(1)}, f32[512,128]{1,0:T(8,128)S(1)}, u32[]{:S(2)}, u32[]{:S(2)}) %collective-permute-start.1) | collective-permute-done | bytes 262176 | tf_op jit(solution)/shard_map/ppermute | solution.py:237
  26.6 6.6 %collective-permute-done.2.c_ref = f32[512,128]{1,0:T(8,128)S(1)} collective-permute-done((f32[512,128]{1,0:T(8,128)S(1)}, f32[512,128]{1,0:T(8,128)S(1)}, u32[]{:S(2)}, u32[]{:S(2)}) %collective-permute-start.2) | collective-permute-done | bytes 262176 | tf_op jit(solution)/shard_map/ppermute | solution.py:237
  33.2 0.0 collective-permute-done.3.d_ref
  33.2 1.0 %outer.1 = f32[8,32,128]{2,1,0:T(8,128)} custom-call(f32[512,128]{1,0:T(8,128)S(1)} %get-tuple-element.8.a_ref, f32[512,128]{1,0:T(8,128)S(1)} %collective-permute-done.1.b_ref, f32[512,128]{1,0:T(8,128)S(1)} %collective-permute-done.2.c_ref, f32[512,128]{1,0:T(8,128)S(1)} %collective-permute-done.3.d_ref), custom_call_target="tpu_custom_call" | custom-call | tf_op jit(solution)/shard_map/outer/pallas_call | solution.py:88
  34.1 3.9 %all-to-all-start = ((f32[8,32,128]{2,1,0:T(8,128)}), f32[8,32,128]{2,1,0:T(8,128)S(1)}, u32[]{:S(2)}, u32[]{:S(2)}) async-start(f32[8,32,128]{2,1,0:T(8,128)} %outer.1), calls=%async_computation | async-start | bytes 262144 | tf_op jit(solution)/shard_map/all_to_all | solution.py:240
  38.1 0.1 pad_add_fusion.place
  38.1 6.1 %all-to-all-done.sums_ref = f32[8,32,128]{2,1,0:T(8,128)S(1)} async-done(((f32[8,32,128]{2,1,0:T(8,128)}), f32[8,32,128]{2,1,0:T(8,128)S(1)}, u32[]{:S(2)}, u32[]{:S(2)}) %all-to-all-start) | async-done | bytes 131104 | tf_op jit(solution)/shard_map/all_to_all | solution.py:240
  44.2 0.7 features.1
  44.9 23.2 %all_to_all.15.got_ref = bf16[32,2,16,128]{3,2,1,0:T(8,128)(2,1)S(1)} all-to-all(bf16[32,2,16,128]{3,2,1,0:T(8,128)(2,1)S(1)} %get-tuple-element.12), channel_id=1, replica_groups=mesh['dp'=32,'tensor'=8] {'dp'}, dimensions={0} | all-to-all | bytes 524288 | tf_op jit(solution)/shard_map/all_to_all | solution.py:243
  68.1 0.0 copy-done.1
  68.1 0.8 score_shares.1
  68.9 4.6 %all-to-all-start.2 = ((f32[32,2,128]{2,1,0:T(2,128)}), f32[32,2,128]{2,1,0:T(2,128)S(1)}, u32[]{:S(2)}, u32[]{:S(2)}) async-start(f32[32,2,128]{2,1,0:T(2,128)} %score_shares.1), calls=%async_computation.2 | async-start | bytes 65536 | tf_op jit(solution)/shard_map/all_to_all | solution.py:244
  73.5 0.1 slice_reduce_fusion
  73.6 1.9 %fisher.1 = f32[128,2,512]{2,1,0:T(2,128)} custom-call(s32[2]{0:T(128)S(1)} %pad_add_fusion.place, bf16[32,2,16,128]{3,2,1,0:T(8,128)(2,1)S(1)} %all_to_all.15.got_ref), custom_call_target="tpu_custom_call" | custom-call | tf_op jit(solution)/shard_map/fisher/pallas_call | solution.py:174
  75.5 6.8 %all-to-all-done.2 = f32[32,2,128]{2,1,0:T(2,128)S(1)} async-done(((f32[32,2,128]{2,1,0:T(2,128)}), f32[32,2,128]{2,1,0:T(2,128)S(1)}, u32[]{:S(2)}, u32[]{:S(2)}) %all-to-all-start.2) | async-done | bytes 32800 | tf_op jit(solution)/shard_map/all_to_all | solution.py:244
  82.4 0.6 broadcast_divide_fusion
  (1 shorter events, 0.0 us)
Async XLA Ops:
  7.9 7.3 %collective-permute-start = (f32[4,512,128]{2,1,0:T(8,128)}, f32[4,512,128]{2,1,0:T(8,128)S(1)}, u32[]{:S(2)}, u32[]{:S(2)}) collective-permute-start(f32[4,512,128]{2,1,0:T(8,128)} %project.3), channel_id=1, source_target_pairs={{0,1},{1,0},{2,3},{3,2},{4,5},{5,4},{6,7},{7,6},{8,9},{9,8},{10,11... | collective-permute-start | bytes 3145736 | tf_op jit(solution)/shard_map/ppermute | solution.py:233
  15.2 1.2 %copy-start = (f32[4,512,128]{2,1,0:T(8,128)S(1)}, f32[4,512,128]{2,1,0:T(8,128)}, u32[]{:S(2)}) copy-start(f32[4,512,128]{2,1,0:T(8,128)} %project.2.own_ref) | copy-start | bytes 3145732
  16.4 51.7 %copy-start.1 = (bf16[2,128,128]{2,1,0:T(8,128)(2,1)S(1)}, bf16[2,128,128]{2,1,0:T(8,128)(2,1)}, u32[]{:S(2)}) copy-start(bf16[2,128,128]{2,1,0:T(8,128)(2,1)} %query_ref.1) | copy-start | bytes 196612
  16.6 10.0 %collective-permute-start.1 = (f32[512,128]{1,0:T(8,128)S(1)}, f32[512,128]{1,0:T(8,128)S(1)}, u32[]{:S(2)}, u32[]{:S(2)}) collective-permute-start(f32[512,128]{1,0:T(8,128)S(1)} %get-tuple-element.9), channel_id=1, source_target_pairs={{0,2},{1,3},{2,4},{3,5},{4,6},{5,7},{6,0},{7,1},{8,10},{9,11},{10,... | collective-permute-start | bytes 786440 | tf_op jit(solution)/shard_map/ppermute | solution.py:237
  18.1 15.0 %collective-permute-start.2 = (f32[512,128]{1,0:T(8,128)S(1)}, f32[512,128]{1,0:T(8,128)S(1)}, u32[]{:S(2)}, u32[]{:S(2)}) collective-permute-start(f32[512,128]{1,0:T(8,128)S(1)} %get-tuple-element.10), channel_id=1, source_target_pairs={{0,4},{1,5},{2,6},{3,7},{4,0},{5,1},{6,2},{7,3},{8,12},{9,13},{10,... | collective-permute-start | bytes 786440 | tf_op jit(solution)/shard_map/ppermute | solution.py:237
  20.9 12.3 %collective-permute-start.3 = (f32[512,128]{1,0:T(8,128)S(1)}, f32[512,128]{1,0:T(8,128)S(1)}, u32[]{:S(2)}, u32[]{:S(2)}) collective-permute-start(f32[512,128]{1,0:T(8,128)S(1)} %get-tuple-element.11), channel_id=1, source_target_pairs={{0,6},{1,7},{2,0},{3,1},{4,2},{5,3},{6,4},{7,5},{8,14},{9,15},{10,... | collective-permute-start | bytes 786440 | tf_op jit(solution)/shard_map/ppermute | solution.py:237
  34.1 10.1 %all-to-all-start = ((f32[8,32,128]{2,1,0:T(8,128)}), f32[8,32,128]{2,1,0:T(8,128)S(1)}, u32[]{:S(2)}, u32[]{:S(2)}) async-start(f32[8,32,128]{2,1,0:T(8,128)} %outer.1), calls=%async_computation | async-start | bytes 262144 | tf_op jit(solution)/shard_map/all_to_all | solution.py:240
  68.9 13.4 %all-to-all-start.2 = ((f32[32,2,128]{2,1,0:T(2,128)}), f32[32,2,128]{2,1,0:T(2,128)S(1)}, u32[]{:S(2)}, u32[]{:S(2)}) async-start(f32[32,2,128]{2,1,0:T(2,128)} %score_shares.1), calls=%async_computation.2 | async-start | bytes 65536 | tf_op jit(solution)/shard_map/all_to_all | solution.py:244

commit v2 on v1

--- a/solution.py
+++ b/solution.py
@@ -20,39 +20,66 @@
     return lax.dot_general(a, b, dims, preferred_element_type=F32)
 
 
-def project_kernel(place, v_ref, a_ref, g_ref, m_ref, wv_ref, wa_ref, wg_ref, wm_ref, out_ref):
-    sequence, block = pl.program_id(0), pl.program_id(1)
-    tokens = v_ref.shape[1]
-    rank = wv_ref.shape[0]
-    rows = pl.ds(pl.multiple_of(block * tokens, tokens), tokens)
-    first = lax.rem(2 * sequence + 4 - place[0], 4)
-    second = lax.rem(2 * sequence + 5 - place[0], 4)
-    out_ref[first, rows, 0:rank] = dot(v_ref[0], wv_ref[...], NT)
-    out_ref[first, rows, rank:LANES] = dot(a_ref[0], wa_ref[...], NT)
-    out_ref[second, rows, 0:rank] = dot(g_ref[0], wg_ref[...], NT)
-    out_ref[second, rows, rank:LANES] = dot(m_ref[0], wm_ref[...], NT)
-
-
-def project(place, acts, weights, tokens):
+def project_kernel(place, v, a, g, m, wv, wa, wg, wm, theirs_ref, own_ref, sv, sa, sg, sm, swv, swa, swg, swm, held, sems, weight_sems):
+    arrays, buffers = (v, a, g, m), (sv, sa, sg, sm)
+    weights, weight_buffers = (wv, wa, wg, wm), (swv, swa, swg, swm)
+    half = v.shape[1] // 2
+    rank = wv.shape[0]
+    chip, core = place[0], place[1]
+
+    def weight_copy(i):
+        return pltpu.make_async_copy(weights[i], weight_buffers[i], weight_sems.at[i])
+
+    def copy(i, chunk):
+        which = lax.rem(core + 1 + chunk // 2, 2)
+        start = pl.multiple_of(which * half, half)
+        return pltpu.make_async_copy(arrays[i].at[chunk % 2, pl.ds(start, half)], buffers[i].at[chunk], sems.at[chunk, i])
+
+    for i in range(4):
+        weight_copy(i).start()
+    for chunk in range(2):
+        for i in range(4):
+            copy(i, chunk).start()
+    for i in range(4):
+        weight_copy(i).wait()
+
+    def work(chunk, carry):
+        for i in range(4):
+            copy(i, chunk).wait()
+
+        @pl.when(chunk < 2)
+        def _():
+            for i in range(4):
+                copy(i, chunk + 2).start()
+
+        for i in range(4):
+            slot = lax.rem(2 * lax.rem(chunk, 2) + i // 2 + 4 - chip, 4)
+            held[chunk // 2, slot, :, (i % 2) * rank : (i % 2 + 1) * rank] = dot(buffers[i][chunk], weight_buffers[i][...], NT)
+        return carry
+
+    lax.fori_loop(0, 4, work, 0)
+    theirs_ref[...] = held[0]
+    own_ref[...] = held[1]
+
+
+def project(place, acts, weights):
     sequences, length, _ = acts[0].shape
     half = length // 2
-    blocks = half // tokens
-    act_specs = [pl.BlockSpec((1, tokens, a.shape[2]), lambda e, b, s: (e, s[1] * blocks + b, 0)) for a in acts]
-    weight_specs = [pl.BlockSpec(w.shape, lambda e, b, s: (0, 0)) for w in weights]
-    flops = 2 * sequences * half * sum(w.size for w in weights)
+    hbm = pl.BlockSpec(memory_space=pltpu.HBM)
+    flops = 2 * sequences * length * sum(w.size for w in weights)
+    held_apart = [pltpu.with_memory_space_constraint(x, pltpu.HBM) for x in (*acts, *weights)]
     return pl.pallas_call(
         project_kernel,
-        grid_spec=pltpu.PrefetchScalarGridSpec(
-            num_scalar_prefetch=1,
-            grid=(sequences, blocks),
-            in_specs=act_specs + weight_specs,
-            out_specs=pl.BlockSpec((4, half, LANES), lambda e, b, s: (0, 0, 0)),
-        ),
-        out_shape=jax.ShapeDtypeStruct((4, half, LANES), F32),
-        cost_estimate=pl.CostEstimate(flops=flops, bytes_accessed=sum(a.size for a in acts) + 4 * half * LANES * 4, transcendentals=0),
-        compiler_params=pltpu.CompilerParams(vmem_limit_bytes=58 * 2**20),
+        out_shape=[pltpu.VMEM((4, half, LANES), F32)] * 2,
+        in_specs=[pl.BlockSpec(memory_space=pltpu.SMEM)] + [hbm] * 8,
+        out_specs=[pl.BlockSpec(memory_space=VMEM)] * 2,
+        scratch_shapes=[pltpu.VMEM((4, half, a.shape[2]), BF16) for a in acts]
+        + [pltpu.VMEM(w.shape, BF16) for w in weights]
+        + [pltpu.VMEM((2, 4, half, LANES), F32), pltpu.SemaphoreType.DMA((4, 4)), pltpu.SemaphoreType.DMA((4,))],
+        cost_estimate=pl.CostEstimate(flops=flops, bytes_accessed=2 * sum(a.size for a in acts), transcendentals=0),
+        compiler_params=pltpu.CompilerParams(vmem_limit_bytes=32 * 2**20),
         name="project",
-    )(place, *acts, *weights)
+    )(place, *held_apart)
 
 
 def add_kernel(own_ref, other_ref, *out_refs):
@@ -61,10 +88,9 @@
 
 
 def add_cores(own, other):
-    shape = jax.ShapeDtypeStruct(own.shape[1:], F32)
     return pl.pallas_call(
         add_kernel,
-        out_shape=[shape] * 4,
+        out_shape=[jax.ShapeDtypeStruct(own.shape[1:], F32)] * 4,
         in_specs=[pl.BlockSpec(memory_space=VMEM)] * 2,
         out_specs=[pl.BlockSpec(memory_space=VMEM)] * 4,
         cost_estimate=pl.CostEstimate(flops=own.size, bytes_accessed=12 * own.size, transcendentals=0),
@@ -96,7 +122,8 @@
     )(*parts)
 
 
-def features_kernel(scale, place, sums_ref, send_ref, norm_ref):
+def features_kernel(scale, place, sums_ref, send_ref, norm_ref, *share_refs):
+    *share_refs, feat_ref = share_refs
     blocks = send_ref.shape[0]
     feats = {}
     squares = {}
@@ -106,10 +133,18 @@
             rounded = ((sums_ref[2 * chip] + sums_ref[2 * chip + 1]) * scale).astype(BF16)
             wide = rounded.astype(F32)
             feats[e, p] = wide
+            feat_ref[e, p] = wide
             squares[e, p] = jnp.sum(jnp.sum(wide * wide, axis=1, keepdims=True), axis=0, keepdims=True)
     for e in range(2):
         mean = (squares[e, 0] + squares[e, 1]) / (2.0 * blocks * LANES)
         norm_ref[e : e + 1, :] = jnp.broadcast_to(jnp.sqrt(mean + 1e-06), (1, LANES))
+    planes = len(share_refs)
+    depth = blocks // planes
+    for turn, share_ref in enumerate(share_refs):
+        start = pl.multiple_of(lax.rem(place[0] // depth + turn, planes) * depth, depth)
+        for e in range(2):
+            for p in range(2):
+                share_ref[e, p * depth : (p + 1) * depth, :] = feat_ref[e, p, pl.ds(start, depth), :]
     row = lax.broadcasted_iota(jnp.int32, (16, LANES), 0)
     for p in range(2):
         total = squares[0, p] + squares[1, p]
@@ -134,16 +169,18 @@
     return (summed * scale).astype(BF16).astype(F32)
 
 
-def features(place, sums, scale, dp):
+def features(place, sums, scale, dp, planes):
     blocks = sums.shape[1]
     return pl.pallas_call(
         functools.partial(features_kernel, scale),
         out_shape=[
             jax.ShapeDtypeStruct((dp, 2, 16, LANES), BF16),
             jax.ShapeDtypeStruct((2, LANES), F32),
-        ],
+        ]
+        + [jax.ShapeDtypeStruct((2, 2 * blocks // planes, LANES), F32)] * planes,
         in_specs=[pl.BlockSpec(memory_space=pltpu.SMEM), pl.BlockSpec(memory_space=VMEM)],
-        out_specs=[pl.BlockSpec(memory_space=VMEM)] * 2,
+        out_specs=[pl.BlockSpec(memory_space=VMEM)] * (2 + planes),
+        scratch_shapes=[pltpu.VMEM((2, 2, blocks, LANES), F32)],
         compiler_params=pltpu.CompilerParams(vmem_limit_bytes=8 * 2**20),
         name="features",
     )(place, sums)
@@ -182,29 +219,43 @@
     )(place, got)
 
 
-def scores_kernel(got_ref, query_ref, out_ref, held):
-    sources = got_ref.shape[0]
+def scores_kernel(distances, place, *refs):
+    queries = len(distances)
+    query_refs, refs = refs[:queries], refs[queries:]
+    planes = (len(refs) - 1) // 2
+    share_refs, out_refs, held = refs[:planes], refs[planes:-1], refs[-1]
+    depth = sum(len(d) for d in distances)
+    z = lax.rem(place[0], depth)
+    rows = 2 * depth
+    for turn, share_ref in enumerate(share_refs):
+        for e in range(2):
+            held[(2 * turn + e) * rows : (2 * turn + e + 1) * rows, :] = share_ref[e]
     total = None
-    for p in range(2):
-        held[...] = got_ref[:, p].astype(F32).reshape(sources * 16, LANES)
-        pair = [held[pl.ds(5 * e, sources, stride=16), :] for e in range(2)]
-        part = dot(jnp.concatenate(pair, axis=0).astype(BF16), query_ref[p], NT)
-        total = part if total is None else total + part
-    out_ref[:, 0, :] = total[0:sources]
-    out_ref[:, 1, :] = total[sources:]
-
-
-def score_shares(got, query):
-    sources = got.shape[0]
-    return pl.pallas_call(
-        scores_kernel,
-        out_shape=jax.ShapeDtypeStruct((sources, 2, query.shape[1]), F32),
-        in_specs=[pl.BlockSpec(memory_space=VMEM)] * 2,
-        out_specs=pl.BlockSpec(memory_space=VMEM),
-        scratch_shapes=[pltpu.VMEM((sources * 16, LANES), F32)],
+    for query_ref, group in zip(query_refs, distances):
+        for at, distance in enumerate(group):
+            source = lax.rem(z + depth - distance, depth)
+            for p in range(2):
+                vectors = held[pl.ds(p * depth + source, 2 * planes, stride=rows), :].astype(BF16)
+                part = dot(vectors, query_ref[at, p], NT)
+                total = part if total is None else total + part
+    for turn, out_ref in enumerate(out_refs):
+        out_ref[...] = total[2 * turn : 2 * turn + 2, :]
+
+
+def score_shares(place, queries, distances, shares):
+    planes = len(shares)
+    vmem = pl.BlockSpec(memory_space=VMEM)
+    size = sum(q.size for q in queries)
+    return pl.pallas_call(
+        functools.partial(scores_kernel, distances),
+        out_shape=[jax.ShapeDtypeStruct((2, queries[0].shape[2]), F32)] * planes,
+        in_specs=[pl.BlockSpec(memory_space=pltpu.SMEM)] + [vmem] * (len(queries) + planes),
+        out_specs=[vmem] * planes,
+        scratch_shapes=[pltpu.VMEM((2 * planes * shares[0].shape[1], LANES), F32)],
+        cost_estimate=pl.CostEstimate(flops=16 * size, bytes_accessed=2 * size, transcendentals=0),
         compiler_params=pltpu.CompilerParams(vmem_limit_bytes=8 * 2**20),
         name="score_shares",
-    )(got, query)
+    )(place, *queries, *shares)
 
 
 def shards(
@@ -227,23 +278,46 @@
     tp_pos = lax.axis_index("tensor")
     chip, core = tp_pos // 2, tp_pos % 2
 
+    planes, depth = 4, dp // 4
+
+    def along_z(x, turn):
+        return lax.ppermute(x, "dp", [(k, k // depth * depth + (k + turn) % depth) for k in range(dp)])
+
+    def along_y(x, turn):
+        return lax.ppermute(x, "dp", [(k, (k + turn * depth) % dp) for k in range(dp)])
+
+    distances, queries = [[0]], [query_features[None]]
+
+    def widen():
+        reach = depth // 2 ** len(queries)
+        queries.append(along_z(jnp.concatenate(queries, axis=0) if len(queries) > 1 else queries[0], reach))
+        distances.append([d + reach for group in distances for d in group])
+
+    widen()
     acts = (v_grad, attn_in, out_grad, mlp_hidden)
     weights = (proj_out_value, proj_in_attn, proj_out_mlp, proj_in_mlp)
-    theirs = project(jnp.stack([chip, 1 - core]).astype(jnp.int32), acts, weights, 256)
+    theirs, own = project(jnp.stack([chip, core]).astype(jnp.int32), acts, weights)
+    theirs, own, queries[1] = lax.optimization_barrier((theirs, own, queries[1]))
     other = lax.ppermute(theirs, "tensor", [(k, k ^ 1) for k in range(width)])
-    own = project(jnp.stack([chip, core]).astype(jnp.int32), acts, weights, 256)
     kept, *sent = add_cores(own, other)
+    widen()
     parts = [kept] + [
         lax.ppermute(sent[s - 1], "tensor", [(k, (k + 2 * s) % width) for k in range(width)]) for s in (1, 2, 3)
     ]
+    parts[2], queries[2] = lax.optimization_barrier((parts[2], queries[2]))
+    widen()
     partial = outer(parts, rank, width)
     sums = lax.all_to_all(partial, "tensor", 0, 0, tiled=True)
+    sums, queries[3] = lax.optimization_barrier((sums, queries[3]))
     place = jnp.stack([dp_pos, tp_pos]).astype(jnp.int32)
-    send, norms = features(place, sums, 1.0 / math.sqrt(length), dp)
+    send, norms, *shares = features(place, sums, 1.0 / math.sqrt(length), dp, planes)
+    shares = [shares[0]] + [along_y(shares[turn], turn) for turn in range(1, planes)]
     got = lax.all_to_all(send, "dp", 0, 0, tiled=True)
-    shares = lax.all_to_all(score_shares(got, query_features), "dp", 0, 0, tiled=True)
+    scored = list(score_shares(place, queries, distances, shares))
+    scored[0], got = lax.optimization_barrier((scored[0], got))
     fisher = fisher_block(place, got, examples)
-    scores = jnp.sum(shares, axis=0) / norms[:, 0:1]
+    scored = [scored[0]] + [along_y(scored[turn], -turn) for turn in range(1, planes)]
+    scores = sum(scored) / norms
     return (fisher, scores)
 
 

time: 83.7 us -> 70.1 us (0.84)
  blocking collectives: 23.2 us -> 0 us
  starting transfers between devices: 14.2 us -> 35.6 us
  Pallas kernels: 17.7 us -> 12.5 us
  waiting for transfers between devices: 23.7 us -> 20.2 us
  local copies, waits for them, and re-layouts: 1.34 us -> 0.01 us
  other arithmetic: 2.06 us -> 0.76 us
    all_to_all x1 -> x0, blocking collectives: 23.2 us -> none  [shards(): got = lax.all_to_all(send, 'dp', 0, 0, tiled=True)]
    ppermute x0 -> x9, starting transfers between devices: none -> 17.9 us  [the longest x6 9.93 us: along_y(): lax.ppermute(x, 'dp', [(k, (k + turn * depth) % dp) for k in range(dp)])]
    ppermute x0 -> x9, waiting for transfers between devices: none -> 9.35 us  [the longest x3 5.47 us: along_z(): lax.ppermute(x, 'dp', [(k, k // depth * depth + (k + turn) % depth) for k...]
    ppermute x3, waiting for transfers between devices: 10.9 us -> 2.13 us  [shards(): lax.ppermute(sent[s - 1], 'tensor', [(k, (k + 2 * s) % width) for k in ra...]
    all_to_all x1, waiting for transfers between devices: 6.79 us -> 0.01 us  [shards(): got = lax.all_to_all(send, 'dp', 0, 0, tiled=True)]
    pallas_call x4 -> x3, Pallas kernels: 14.2 us -> 8.24 us  [the longest x1 7.24 us: project(): pl.pallas_call(project_kernel, out_shape=[pltpu.VMEM((4, half, LANES), F3...]
    ppermute x1, waiting for transfers between devices: 0.01 us -> 2.65 us  [shards(): other = lax.ppermute(theirs, 'tensor', [(k, k ^ 1) for k in range(width)])]
    all_to_all x1, starting transfers between devices: 4.56 us -> 7 us  [shards(): got = lax.all_to_all(send, 'dp', 0, 0, tiled=True)]
  transfers between devices with their start and end apart: 6 -> 15, of which waited for: 4 -> 8; matrix products, arithmetic and copies ran while one was open for 1% -> 0% of each run, Pallas kernels for 10% -> 16%
where the time goes in v2:
time: 70.1 us; the launch traced here: 69.8 us
  starting transfers between devices  35.6 us (51%)
  waiting for transfers between devices  20.2 us (29%)
  Pallas kernels  12.5 us (18%)
  other arithmetic  0.76 us (1%)
    ppermute x6, starting transfers between devices, along_y(): lax.ppermute(x, 'dp', [(k, (k + turn * depth) % dp) for k in range(dp)])  9.93 us
    ppermute x3, starting transfers between devices, along_z(): lax.ppermute(x, 'dp', [(k, k // depth * depth + (k + turn) % depth) for k...  8.01 us
    pallas_call x1, Pallas kernels, project(): pl.pallas_call(project_kernel, out_shape=[pltpu.VMEM((4, half, LANES), F3...  7.24 us
    all_to_all x1, starting transfers between devices, shards(): got = lax.all_to_all(send, 'dp', 0, 0, tiled=True)  7 us
    ppermute x3, starting transfers between devices, shards(): lax.ppermute(sent[s - 1], 'tensor', [(k, (k + 2 * s) % width) for k in ra...  6.35 us
    all_to_all x1, waiting for transfers between devices, shards(): sums = lax.all_to_all(partial, 'tensor', 0, 0, tiled=True)  6.06 us
    ppermute x3, waiting for transfers between devices, along_z(): lax.ppermute(x, 'dp', [(k, k // depth * depth + (k + turn) % depth) for k...  5.47 us
    all_to_all x1, starting transfers between devices, shards(): sums = lax.all_to_all(partial, 'tensor', 0, 0, tiled=True)  4.22 us
  transfers between devices with their start and end apart: 15, of which 8 were waited for; matrix products, arithmetic and copies ran while one was open for 0% of the time, Pallas kernels for 16%

profile of v2, /device:TPU:32, one launch (start us, length us, event | category | flops | bytes accessed | tf_op | source)
XLA Modules:
  0.0 69.8 jit_solution(675798929588379621)
XLA Ops:
  0.6 6.4 %collective-permute-start = (bf16[1,2,128,128]{3,2,1,0:T(8,128)(2,1)}, bf16[1,2,128,128]{3,2,1,0:T(8,128)(2,1)S(1)}, u32[]{:S(2)}, u32[]{:S(2)}) collective-permute-start(bf16[1,2,128,128]{3,2,1,0:T(8,128)(2,1)} %bitcast.5), channel_id=1, source_target_pairs={{0,32},{8,40},{16,48},{24,56},{32,0},{40,8},{48,16},{56,24},{64,96... | collective-permute-start | bytes 196616 | tf_op jit(solution)/shard_map/ppermute | solution.py:284
  7.0 0.1 pad_add_fusion.1.place
  7.1 7.2 %project.1 = (f32[4,512,128]{2,1,0:T(8,128)S(1)}, f32[4,512,128]{2,1,0:T(8,128)S(1)}) custom-call(s32[2]{0:T(128)S(1)} %pad_add_fusion.1.place, bf16[2,1024,128]{2,1,0:T(8,128)(2,1)} %v.1, bf16[2,1024,512]{2,1,0:T(8,128)(2,1)} %a.1, bf16[2,1024,512]{2,1,0:T(8,128)(2,1)} %g.1, bf16[2,1024,1792]{2,1,0:T(8,128)(2,1)} %m.1, bf16[64,128]{1,0:T(8,128)(2,1)} %wv.1, ...), custom_call_target="tpu_custom_call" | custom-call | flops 771751936 | bytes 12058624 | tf_op jit(solution)/shard_map/project/pallas_call | solution.py:71
  14.3 0.0 copy-start
  14.3 0.0 collective-permute-done.refs_1_
  14.4 0.1 collective-permute-start.1
  14.5 2.6 %collective-permute-done.1.other_ref = f32[4,512,128]{2,1,0:T(8,128)S(1)} collective-permute-done((f32[4,512,128]{2,1,0:T(8,128)S(1)}, f32[4,512,128]{2,1,0:T(8,128)S(1)}, u32[]{:S(2)}, u32[]{:S(2)}) %collective-permute-start.1) | collective-permute-done | bytes 1048608 | tf_op jit(solution)/shard_map/ppermute | solution.py:301
  17.1 0.1 add_cores.1
  17.2 3.1 %collective-permute-start.2 = (f32[512,128]{1,0:T(8,128)S(1)}, f32[512,128]{1,0:T(8,128)S(1)}, u32[]{:S(2)}, u32[]{:S(2)}) collective-permute-start(f32[512,128]{1,0:T(8,128)S(1)} %get-tuple-element.32), channel_id=1, source_target_pairs={{0,4},{1,5},{2,6},{3,7},{4,0},{5,1},{6,2},{7,3},{8,12},{9,13},{10,... | collective-permute-start | bytes 786440 | tf_op jit(solution)/shard_map/ppermute | solution.py:305
  20.3 0.0 copy-done
  20.3 1.5 %collective-permute-start.3 = (bf16[2,2,128,128]{3,2,1,0:T(8,128)(2,1)S(1)}, bf16[2,2,128,128]{3,2,1,0:T(8,128)(2,1)S(1)}, u32[]{:S(2)}, u32[]{:S(2)}) collective-permute-start(bf16[2,2,128,128]{3,2,1,0:T(8,128)(2,1)S(1)} %pad_maximum_fusion.1), channel_id=1, source_target_pairs={{0,16},{8,24},{16,32},{24,40},{32,48},{40,56},{48,0},{56,8},{64,80... | collective-permute-start | bytes 393224 | tf_op jit(solution)/shard_map/ppermute | solution.py:284
  21.9 0.6 collective-permute-start.4
  22.5 2.6 %collective-permute-start.5 = (f32[512,128]{1,0:T(8,128)S(1)}, f32[512,128]{1,0:T(8,128)S(1)}, u32[]{:S(2)}, u32[]{:S(2)}) collective-permute-start(f32[512,128]{1,0:T(8,128)S(1)} %get-tuple-element.37), channel_id=1, source_target_pairs={{0,6},{1,7},{2,0},{3,1},{4,2},{5,3},{6,4},{7,5},{8,14},{9,15},{10,... | collective-permute-start | bytes 786440 | tf_op jit(solution)/shard_map/ppermute | solution.py:305
  25.1 5.5 %collective-permute-done.3.refs_2_ = bf16[2,2,128,128]{3,2,1,0:T(8,128)(2,1)S(1)} collective-permute-done((bf16[2,2,128,128]{3,2,1,0:T(8,128)(2,1)S(1)}, bf16[2,2,128,128]{3,2,1,0:T(8,128)(2,1)S(1)}, u32[]{:S(2)}, u32[]{:S(2)}) %collective-permute-start.3) | collective-permute-done | bytes 131104 | tf_op jit(solution)/shard_map/ppermute | solution.py:284
  30.6 0.0 collective-permute-done.2.c_ref
  30.6 0.1 collective-permute-start.6
  30.7 2.0 %collective-permute-done.4.b_ref = f32[512,128]{1,0:T(8,128)S(1)} collective-permute-done((f32[512,128]{1,0:T(8,128)S(1)}, f32[512,128]{1,0:T(8,128)S(1)}, u32[]{:S(2)}, u32[]{:S(2)}) %collective-permute-start.4) | collective-permute-done | bytes 262176 | tf_op jit(solution)/shard_map/ppermute | solution.py:305
  32.8 0.1 collective-permute-done.5.d_ref
  32.9 1.0 %outer.1 = f32[8,32,128]{2,1,0:T(8,128)} custom-call(f32[512,128]{1,0:T(8,128)S(1)} %get-tuple-element.34.a_ref, f32[512,128]{1,0:T(8,128)S(1)} %collective-permute-done.4.b_ref, f32[512,128]{1,0:T(8,128)S(1)} %collective-permute-done.2.c_ref, f32[512,128]{1,0:T(8,128)S(1)} %collective-permute-done.5.d_ref), custom_call_target="tpu_custom_call" | custom-call | tf_op jit(solution)/shard_map/outer/pallas_call | solution.py:114
  33.8 4.2 %all-to-all-start = ((f32[8,32,128]{2,1,0:T(8,128)}), f32[8,32,128]{2,1,0:T(8,128)S(1)}, u32[]{:S(2)}, u32[]{:S(2)}) async-start(f32[8,32,128]{2,1,0:T(8,128)} %outer.1), calls=%async_computation | async-start | bytes 262144 | tf_op jit(solution)/shard_map/all_to_all | solution.py:310
  38.0 0.1 pad_add_fusion.place
  38.1 6.1 %all-to-all-done.sums_ref = f32[8,32,128]{2,1,0:T(8,128)S(1)} async-done(((f32[8,32,128]{2,1,0:T(8,128)}), f32[8,32,128]{2,1,0:T(8,128)S(1)}, u32[]{:S(2)}, u32[]{:S(2)}) %all-to-all-start) | async-done | bytes 131104 | tf_op jit(solution)/shard_map/all_to_all | solution.py:310
  44.2 0.0 collective-permute-done.6.refs_3_
  44.2 1.4 %features.1 = (bf16[32,2,16,128]{3,2,1,0:T(8,128)(2,1)}, f32[2,128]{1,0:T(2,128)S(1)}, f32[2,16,128]{2,1,0:T(8,128)S(1)}, f32[2,16,128]{2,1,0:T(8,128)S(1)}, f32...) custom-call(s32[2]{0:T(128)S(1)} %pad_add_fusion.place, f32[8,32,128]{2,1,0:T(8,128)S(1)} %all-to-all-done.sums_ref), custom_call_target="tpu_custom_call" | custom-call | tf_op jit(solution)/shard_map/features/pallas_call | solution.py:174
  45.6 7.0 %all-to-all-start.1 = ((bf16[32,2,16,128]{3,2,1,0:T(8,128)(2,1)}), bf16[32,2,16,128]{3,2,1,0:T(8,128)(2,1)S(1)}, u32[]{:S(2)}, u32[]{:S(2)}) async-start(bf16[32,2,16,128]{3,2,1,0:T(8,128)(2,1)} %get-tuple-element.45), calls=%async_computation.1 | async-start | bytes 524288 | tf_op jit(solution)/shard_map/all_to_all | solution.py:315
  52.6 1.5 %collective-permute-start.7 = (f32[2,16,128]{2,1,0:T(8,128)S(1)}, f32[2,16,128]{2,1,0:T(8,128)S(1)}, u32[]{:S(2)}, u32[]{:S(2)}) collective-permute-start(f32[2,16,128]{2,1,0:T(8,128)S(1)} %get-tuple-element.41), channel_id=1, source_target_pairs={{0,64},{8,72},{16,80},{24,88},{32,96},{40,104},{48,112},{56,120},{... | collective-permute-start | bytes 49160 | tf_op jit(solution)/shard_map/ppermute | solution.py:287
  54.1 2.7 %collective-permute-start.8 = (f32[2,16,128]{2,1,0:T(8,128)S(1)}, f32[2,16,128]{2,1,0:T(8,128)S(1)}, u32[]{:S(2)}, u32[]{:S(2)}) collective-permute-start(f32[2,16,128]{2,1,0:T(8,128)S(1)} %get-tuple-element.42), channel_id=1, source_target_pairs={{0,128},{8,136},{16,144},{24,152},{32,160},{40,168},{48,176},{56,1... | collective-permute-start | bytes 49160 | tf_op jit(solution)/shard_map/ppermute | solution.py:287
  56.8 1.4 %collective-permute-start.9 = (f32[2,16,128]{2,1,0:T(8,128)S(1)}, f32[2,16,128]{2,1,0:T(8,128)S(1)}, u32[]{:S(2)}, u32[]{:S(2)}) collective-permute-start(f32[2,16,128]{2,1,0:T(8,128)S(1)} %get-tuple-element.43), channel_id=1, source_target_pairs={{0,192},{8,200},{16,208},{24,216},{32,224},{40,232},{48,240},{56,2... | collective-permute-start | bytes 49160 | tf_op jit(solution)/shard_map/ppermute | solution.py:287
  58.3 0.0 collective-permute-done.7.refs_5_
  58.3 1.2 %collective-permute-done.8.refs_6_ = f32[2,16,128]{2,1,0:T(8,128)S(1)} collective-permute-done((f32[2,16,128]{2,1,0:T(8,128)S(1)}, f32[2,16,128]{2,1,0:T(8,128)S(1)}, u32[]{:S(2)}, u32[]{:S(2)}) %collective-permute-start.8) | collective-permute-done | bytes 16416 | tf_op jit(solution)/shard_map/ppermute | solution.py:287
  59.4 1.2 %collective-permute-done.9.refs_7_ = f32[2,16,128]{2,1,0:T(8,128)S(1)} collective-permute-done((f32[2,16,128]{2,1,0:T(8,128)S(1)}, f32[2,16,128]{2,1,0:T(8,128)S(1)}, u32[]{:S(2)}, u32[]{:S(2)}) %collective-permute-start.9) | collective-permute-done | bytes 16416 | tf_op jit(solution)/shard_map/ppermute | solution.py:287
  60.6 0.9 %score_shares.1 = (f32[2,128]{1,0:T(2,128)S(1)}, f32[2,128]{1,0:T(2,128)S(1)}, f32[2,128]{1,0:T(2,128)S(1)}, f32[2,128]{1,0:T(2,128)S(1)}) custom-call(s32[2]{0:T(128)S(1)} %pad_add_fusion.place, bf16[1,2,128,128]{3,2,1,0:T(8,128)(2,1)S(1)} %bitcast.8, bf16[1,2,128,128]{3,2,1,0:T(8,128)(2,1)S(1)} %collective-permute-done.refs_1_, ...), custom_call_target="tpu_custom_call" | custom-call | flops 4194304 | bytes 524288 | tf_op jit(solution)/shard_map/score_shares/pallas_call | solution.py:249
  61.5 0.3 collective-permute-start.12
  61.8 3.9 %collective-permute-start.11 = (f32[2,128]{1,0:T(2,128)S(1)}, f32[2,128]{1,0:T(2,128)S(1)}, u32[]{:S(2)}, u32[]{:S(2)}) collective-permute-start(f32[2,128]{1,0:T(2,128)S(1)} %get-tuple-element.49), channel_id=1, source_target_pairs={{0,128},{8,136},{16,144},{24,152},{32,160},{40,168},{48,176},{56,1... | collective-permute-start | bytes 3080 | tf_op jit(solution)/shard_map/ppermute | solution.py:287
  65.6 0.1 collective-permute-start.10
  65.7 0.0 all-to-all-done.1.got_ref
  65.7 1.9 %fisher.1 = f32[128,2,512]{2,1,0:T(2,128)} custom-call(s32[2]{0:T(128)S(1)} %pad_add_fusion.place, bf16[32,2,16,128]{3,2,1,0:T(8,128)(2,1)S(1)} %all-to-all-done.1.got_ref), custom_call_target="tpu_custom_call" | custom-call | tf_op jit(solution)/shard_map/fisher/pallas_call | solution.py:211
  67.7 0.0 collective-permute-done.12
  67.7 0.0 collective-permute-done.11
  67.7 1.5 %collective-permute-done.10 = f32[2,128]{1,0:T(2,128)S(1)} collective-permute-done((f32[2,128]{1,0:T(2,128)S(1)}, f32[2,128]{1,0:T(2,128)S(1)}, u32[]{:S(2)}, u32[]{:S(2)}) %collective-permute-start.10) | collective-permute-done | bytes 1056 | tf_op jit(solution)/shard_map/ppermute | solution.py:287
  69.2 0.6 add_divide_fusion
  (2 shorter events, 0.0 us)
Async XLA Ops:
  0.6 13.7 %collective-permute-start = (bf16[1,2,128,128]{3,2,1,0:T(8,128)(2,1)}, bf16[1,2,128,128]{3,2,1,0:T(8,128)(2,1)S(1)}, u32[]{:S(2)}, u32[]{:S(2)}) collective-permute-start(bf16[1,2,128,128]{3,2,1,0:T(8,128)(2,1)} %bitcast.5), channel_id=1, source_target_pairs={{0,32},{8,40},{16,48},{24,56},{32,0},{40,8},{48,16},{56,24},{64,96... | collective-permute-start | bytes 196616 | tf_op jit(solution)/shard_map/ppermute | solution.py:284
  14.3 6.0 %copy-start = (bf16[2,128,128]{2,1,0:T(8,128)(2,1)S(1)}, bf16[2,128,128]{2,1,0:T(8,128)(2,1)}, u32[]{:S(2)}) copy-start(bf16[2,128,128]{2,1,0:T(8,128)(2,1)} %param.17) | copy-start | bytes 196612
  14.4 2.7 %collective-permute-start.1 = (f32[4,512,128]{2,1,0:T(8,128)S(1)}, f32[4,512,128]{2,1,0:T(8,128)S(1)}, u32[]{:S(2)}, u32[]{:S(2)}) collective-permute-start(f32[4,512,128]{2,1,0:T(8,128)S(1)} %get-tuple-element.31), channel_id=1, source_target_pairs={{0,1},{1,0},{2,3},{3,2},{4,5},{5,4},{6,7},{7,6},{8,9},{9,8},{10,11... | collective-permute-start | bytes 3145736 | tf_op jit(solution)/shard_map/ppermute | solution.py:301
  17.2 13.4 %collective-permute-start.2 = (f32[512,128]{1,0:T(8,128)S(1)}, f32[512,128]{1,0:T(8,128)S(1)}, u32[]{:S(2)}, u32[]{:S(2)}) collective-permute-start(f32[512,128]{1,0:T(8,128)S(1)} %get-tuple-element.32), channel_id=1, source_target_pairs={{0,4},{1,5},{2,6},{3,7},{4,0},{5,1},{6,2},{7,3},{8,12},{9,13},{10,... | collective-permute-start | bytes 786440 | tf_op jit(solution)/shard_map/ppermute | solution.py:305
  20.3 10.3 %collective-permute-start.3 = (bf16[2,2,128,128]{3,2,1,0:T(8,128)(2,1)S(1)}, bf16[2,2,128,128]{3,2,1,0:T(8,128)(2,1)S(1)}, u32[]{:S(2)}, u32[]{:S(2)}) collective-permute-start(bf16[2,2,128,128]{3,2,1,0:T(8,128)(2,1)S(1)} %pad_maximum_fusion.1), channel_id=1, source_target_pairs={{0,16},{8,24},{16,32},{24,40},{32,48},{40,56},{48,0},{56,8},{64,80... | collective-permute-start | bytes 393224 | tf_op jit(solution)/shard_map/ppermute | solution.py:284
  21.9 10.9 %collective-permute-start.4 = (f32[512,128]{1,0:T(8,128)S(1)}, f32[512,128]{1,0:T(8,128)S(1)}, u32[]{:S(2)}, u32[]{:S(2)}) collective-permute-start(f32[512,128]{1,0:T(8,128)S(1)} %get-tuple-element.35), channel_id=1, source_target_pairs={{0,2},{1,3},{2,4},{3,5},{4,6},{5,7},{6,0},{7,1},{8,10},{9,11},{10,... | collective-permute-start | bytes 786440 | tf_op jit(solution)/shard_map/ppermute | solution.py:305
  22.5 10.4 %collective-permute-start.5 = (f32[512,128]{1,0:T(8,128)S(1)}, f32[512,128]{1,0:T(8,128)S(1)}, u32[]{:S(2)}, u32[]{:S(2)}) collective-permute-start(f32[512,128]{1,0:T(8,128)S(1)} %get-tuple-element.37), channel_id=1, source_target_pairs={{0,6},{1,7},{2,0},{3,1},{4,2},{5,3},{6,4},{7,5},{8,14},{9,15},{10,... | collective-permute-start | bytes 786440 | tf_op jit(solution)/shard_map/ppermute | solution.py:305
  30.6 13.5 %collective-permute-start.6 = (bf16[4,2,128,128]{3,2,1,0:T(8,128)(2,1)S(1)}, bf16[4,2,128,128]{3,2,1,0:T(8,128)(2,1)S(1)}, u32[]{:S(2)}, u32[]{:S(2)}) collective-permute-start(bf16[4,2,128,128]{3,2,1,0:T(8,128)(2,1)S(1)} %pad_maximum_fusion), channel_id=1, source_target_pairs={{0,8},{8,16},{16,24},{24,32},{32,40},{40,48},{48,56},{56,0},{64,72... | collective-permute-start | bytes 786440 | tf_op jit(solution)/shard_map/ppermute | solution.py:284
  33.8 10.4 %all-to-all-start = ((f32[8,32,128]{2,1,0:T(8,128)}), f32[8,32,128]{2,1,0:T(8,128)S(1)}, u32[]{:S(2)}, u32[]{:S(2)}) async-start(f32[8,32,128]{2,1,0:T(8,128)} %outer.1), calls=%async_computation | async-start | bytes 262144 | tf_op jit(solution)/shard_map/all_to_all | solution.py:310
  45.6 20.2 %all-to-all-start.1 = ((bf16[32,2,16,128]{3,2,1,0:T(8,128)(2,1)}), bf16[32,2,16,128]{3,2,1,0:T(8,128)(2,1)S(1)}, u32[]{:S(2)}, u32[]{:S(2)}) async-start(bf16[32,2,16,128]{3,2,1,0:T(8,128)(2,1)} %get-tuple-element.45), calls=%async_computation.1 | async-start | bytes 524288 | tf_op jit(solution)/shard_map/all_to_all | solution.py:315
  52.6 5.7 %collective-permute-start.7 = (f32[2,16,128]{2,1,0:T(8,128)S(1)}, f32[2,16,128]{2,1,0:T(8,128)S(1)}, u32[]{:S(2)}, u32[]{:S(2)}) collective-permute-start(f32[2,16,128]{2,1,0:T(8,128)S(1)} %get-tuple-element.41), channel_id=1, source_target_pairs={{0,64},{8,72},{16,80},{24,88},{32,96},{40,104},{48,112},{56,120},{... | collective-permute-start | bytes 49160 | tf_op jit(solution)/shard_map/ppermute | solution.py:287
  54.1 5.3 %collective-permute-start.8 = (f32[2,16,128]{2,1,0:T(8,128)S(1)}, f32[2,16,128]{2,1,0:T(8,128)S(1)}, u32[]{:S(2)}, u32[]{:S(2)}) collective-permute-start(f32[2,16,128]{2,1,0:T(8,128)S(1)} %get-tuple-element.42), channel_id=1, source_target_pairs={{0,128},{8,136},{16,144},{24,152},{32,160},{40,168},{48,176},{56,1... | collective-permute-start | bytes 49160 | tf_op jit(solution)/shard_map/ppermute | solution.py:287
  56.8 3.8 %collective-permute-start.9 = (f32[2,16,128]{2,1,0:T(8,128)S(1)}, f32[2,16,128]{2,1,0:T(8,128)S(1)}, u32[]{:S(2)}, u32[]{:S(2)}) collective-permute-start(f32[2,16,128]{2,1,0:T(8,128)S(1)} %get-tuple-element.43), channel_id=1, source_target_pairs={{0,192},{8,200},{16,208},{24,216},{32,224},{40,232},{48,240},{56,2... | collective-permute-start | bytes 49160 | tf_op jit(solution)/shard_map/ppermute | solution.py:287
  61.5 6.2 %collective-permute-start.12 = (f32[2,128]{1,0:T(2,128)S(1)}, f32[2,128]{1,0:T(2,128)S(1)}, u32[]{:S(2)}, u32[]{:S(2)}) collective-permute-start(f32[2,128]{1,0:T(2,128)S(1)} %get-tuple-element.50), channel_id=1, source_target_pairs={{0,64},{8,72},{16,80},{24,88},{32,96},{40,104},{48,112},{56,120},{... | collective-permute-start | bytes 3080 | tf_op jit(solution)/shard_map/ppermute | solution.py:287
  61.8 5.9 %collective-permute-start.11 = (f32[2,128]{1,0:T(2,128)S(1)}, f32[2,128]{1,0:T(2,128)S(1)}, u32[]{:S(2)}, u32[]{:S(2)}) collective-permute-start(f32[2,128]{1,0:T(2,128)S(1)} %get-tuple-element.49), channel_id=1, source_target_pairs={{0,128},{8,136},{16,144},{24,152},{32,160},{40,168},{48,176},{56,1... | collective-permute-start | bytes 3080 | tf_op jit(solution)/shard_map/ppermute | solution.py:287
  65.6 3.6 %collective-permute-start.10 = (f32[2,128]{1,0:T(2,128)S(1)}, f32[2,128]{1,0:T(2,128)S(1)}, u32[]{:S(2)}, u32[]{:S(2)}) collective-permute-start(f32[2,128]{1,0:T(2,128)S(1)} %get-tuple-element.48), channel_id=1, source_target_pairs={{0,192},{8,200},{16,208},{24,216},{32,224},{40,232},{48,240},{56,2... | collective-permute-start | bytes 3080 | tf_op jit(solution)/shard_map/ppermute | solution.py:287

commit v3 on v2

--- a/solution.py
+++ b/solution.py
@@ -20,20 +20,25 @@
     return lax.dot_general(a, b, dims, preferred_element_type=F32)
 
 
-def project_kernel(place, v, a, g, m, wv, wa, wg, wm, theirs_ref, own_ref, sv, sa, sg, sm, swv, swa, swg, swm, held, sems, weight_sems):
-    arrays, buffers = (v, a, g, m), (sv, sa, sg, sm)
-    weights, weight_buffers = (wv, wa, wg, wm), (swv, swa, swg, swm)
+def project_kernel(place, v, a, g, m, wv, wa, wg, wm, theirs_ref, own_ref, value, down, value_weights, down_weights, sems, weight_sems):
+    arrays, buffers = (v, a, g, m), (value, value, down, down)
+    weights, weight_buffers = (wv, wa, wg, wm), (value_weights, value_weights, down_weights, down_weights)
     half = v.shape[1] // 2
     rank = wv.shape[0]
     chip, core = place[0], place[1]
 
+    def columns(i):
+        return pl.ds(0, arrays[i].shape[2]) if i % 2 == 0 else pl.ds(arrays[i - 1].shape[2], arrays[i].shape[2])
+
     def weight_copy(i):
-        return pltpu.make_async_copy(weights[i], weight_buffers[i], weight_sems.at[i])
+        target = weight_buffers[i].at[pl.ds(i % 2 * rank, rank), columns(i)]
+        return pltpu.make_async_copy(weights[i], target, weight_sems.at[i])
 
     def copy(i, chunk):
         which = lax.rem(core + 1 + chunk // 2, 2)
         start = pl.multiple_of(which * half, half)
-        return pltpu.make_async_copy(arrays[i].at[chunk % 2, pl.ds(start, half)], buffers[i].at[chunk], sems.at[chunk, i])
+        target = buffers[i].at[chunk, :, columns(i)]
+        return pltpu.make_async_copy(arrays[i].at[chunk % 2, pl.ds(start, half)], target, sems.at[chunk, i])
 
     for i in range(4):
         weight_copy(i).start()
@@ -41,9 +46,11 @@
         for i in range(4):
             copy(i, chunk).start()
     for i in range(4):
+        weight_buffers[i][pl.ds((1 - i % 2) * rank, rank), columns(i)] = jnp.zeros((rank, arrays[i].shape[2]), BF16)
+    for i in range(4):
         weight_copy(i).wait()
 
-    def work(chunk, carry):
+    def work(out_ref, chunk, carry):
         for i in range(4):
             copy(i, chunk).wait()
 
@@ -52,30 +59,31 @@
             for i in range(4):
                 copy(i, chunk + 2).start()
 
-        for i in range(4):
-            slot = lax.rem(2 * lax.rem(chunk, 2) + i // 2 + 4 - chip, 4)
-            held[chunk // 2, slot, :, (i % 2) * rank : (i % 2 + 1) * rank] = dot(buffers[i][chunk], weight_buffers[i][...], NT)
+        for p, (inputs, matrix) in enumerate(((value, value_weights), (down, down_weights))):
+            slot = lax.rem(2 * lax.rem(chunk, 2) + p + 4 - chip, 4)
+            out_ref[slot] = dot(inputs[chunk], matrix[...], NT)
         return carry
 
-    lax.fori_loop(0, 4, work, 0)
-    theirs_ref[...] = held[0]
-    own_ref[...] = held[1]
+    lax.fori_loop(0, 2, functools.partial(work, theirs_ref), 0)
+    lax.fori_loop(2, 4, functools.partial(work, own_ref), 0)
 
 
 def project(place, acts, weights):
     sequences, length, _ = acts[0].shape
     half = length // 2
+    rank = weights[0].shape[0]
     hbm = pl.BlockSpec(memory_space=pltpu.HBM)
     flops = 2 * sequences * length * sum(w.size for w in weights)
     held_apart = [pltpu.with_memory_space_constraint(x, pltpu.HBM) for x in (*acts, *weights)]
+    widths = [acts[0].shape[2] + acts[1].shape[2], acts[2].shape[2] + acts[3].shape[2]]
     return pl.pallas_call(
         project_kernel,
         out_shape=[pltpu.VMEM((4, half, LANES), F32)] * 2,
         in_specs=[pl.BlockSpec(memory_space=pltpu.SMEM)] + [hbm] * 8,
         out_specs=[pl.BlockSpec(memory_space=VMEM)] * 2,
-        scratch_shapes=[pltpu.VMEM((4, half, a.shape[2]), BF16) for a in acts]
-        + [pltpu.VMEM(w.shape, BF16) for w in weights]
-        + [pltpu.VMEM((2, 4, half, LANES), F32), pltpu.SemaphoreType.DMA((4, 4)), pltpu.SemaphoreType.DMA((4,))],
+        scratch_shapes=[pltpu.VMEM((4, half, width), BF16) for width in widths]
+        + [pltpu.VMEM((2 * rank, width), BF16) for width in widths]
+        + [pltpu.SemaphoreType.DMA((4, 4)), pltpu.SemaphoreType.DMA((4,))],
         cost_estimate=pl.CostEstimate(flops=flops, bytes_accessed=2 * sum(a.size for a in acts), transcendentals=0),
         compiler_params=pltpu.CompilerParams(vmem_limit_bytes=32 * 2**20),
         name="project",
@@ -113,7 +121,7 @@
 def outer(parts, rank, width):
     return pl.pallas_call(
         functools.partial(outer_kernel, rank),
-        out_shape=jax.ShapeDtypeStruct((width, rank // 2, LANES), F32),
+        out_shape=pltpu.VMEM((width, rank // 2, LANES), F32),
         in_specs=[pl.BlockSpec(memory_space=VMEM)] * 4,
         out_specs=pl.BlockSpec(memory_space=VMEM),
         scratch_shapes=[pltpu.VMEM((rank, LANES), F32)],
@@ -141,7 +149,7 @@
     planes = len(share_refs)
     depth = blocks // planes
     for turn, share_ref in enumerate(share_refs):
-        start = pl.multiple_of(lax.rem(place[0] // depth + turn, planes) * depth, depth)
+        start = pl.multiple_of(lax.rem(place[2] // depth + turn, planes) * depth, depth)
         for e in range(2):
             for p in range(2):
                 share_ref[e, p * depth : (p + 1) * depth, :] = feat_ref[e, p, pl.ds(start, depth), :]
@@ -154,7 +162,7 @@
         base = jnp.zeros((16, LANES), F32)
         for e in range(2):
             for k in range(4):
-                at = place[1] * 4 + k
+                at = place[3] * 4 + k
                 base = jnp.where(row == 5 * e + 1 + k, rounded_row(sums_ref, scale, 2 * e + p, at), base)
         for k, term in enumerate((high, middle, low)):
             base = jnp.where(row == 10 + k, term, base)
@@ -174,10 +182,10 @@
     return pl.pallas_call(
         functools.partial(features_kernel, scale),
         out_shape=[
-            jax.ShapeDtypeStruct((dp, 2, 16, LANES), BF16),
-            jax.ShapeDtypeStruct((2, LANES), F32),
+            pltpu.VMEM((dp, 2, 16, LANES), BF16),
+            pltpu.VMEM((2, LANES), F32),
         ]
-        + [jax.ShapeDtypeStruct((2, 2 * blocks // planes, LANES), F32)] * planes,
+        + [pltpu.VMEM((2, 2 * blocks // planes, LANES), F32)] * planes,
         in_specs=[pl.BlockSpec(memory_space=pltpu.SMEM), pl.BlockSpec(memory_space=VMEM)],
         out_specs=[pl.BlockSpec(memory_space=VMEM)] * (2 + planes),
         scratch_shapes=[pltpu.VMEM((2, 2, blocks, LANES), F32)],
@@ -198,25 +206,27 @@
             return held[pl.ds(r, sources, stride=16), :]
 
         mine = jnp.concatenate([pick(0), pick(5)], axis=0).astype(BF16)
+        theirs = [jnp.concatenate([pick(1 + k), pick(6 + k)], axis=0) for k in range(4)]
         total = jnp.sum(pick(10) + pick(11) + pick(12), axis=0, keepdims=True)
         damping = 0.5 * total / count
+        blocks = dot(mine, jnp.concatenate(theirs, axis=1).astype(BF16), TN) * (1.0 / examples)
         for k in range(4):
-            theirs = jnp.concatenate([pick(1 + k), pick(6 + k)], axis=0).astype(BF16)
-            block = dot(mine, theirs, TN) * (1.0 / examples)
-            on = jnp.logical_and(row == lane, place[0] - 4 * place[1] == k)
-            out_ref[:, p, k * LANES : (k + 1) * LANES] = block + jnp.where(on, damping, 0.0)
+            on = jnp.logical_and(row == lane, place[2] - 4 * place[3] == k)
+            made = blocks[:, k * LANES : (k + 1) * LANES] + jnp.where(on, damping, 0.0)
+            out_ref[pl.ds(2 * k + p, LANES, stride=8), :] = made
 
 
 def fisher_block(place, got, examples):
-    return pl.pallas_call(
+    made = pl.pallas_call(
         functools.partial(fisher_kernel, examples),
-        out_shape=jax.ShapeDtypeStruct((LANES, 2, 4 * LANES), F32),
+        out_shape=jax.ShapeDtypeStruct((8 * LANES, LANES), F32),
         in_specs=[pl.BlockSpec(memory_space=pltpu.SMEM), pl.BlockSpec(memory_space=VMEM)],
         out_specs=pl.BlockSpec(memory_space=VMEM),
         scratch_shapes=[pltpu.VMEM((got.shape[0] * 16, LANES), F32)],
         compiler_params=pltpu.CompilerParams(vmem_limit_bytes=8 * 2**20),
         name="fisher",
     )(place, got)
+    return made.reshape(LANES, 4, 2, LANES).transpose(0, 2, 1, 3).reshape(LANES, 2, 4 * LANES)
 
 
 def scores_kernel(distances, place, *refs):
@@ -225,7 +235,7 @@
     planes = (len(refs) - 1) // 2
     share_refs, out_refs, held = refs[:planes], refs[planes:-1], refs[-1]
     depth = sum(len(d) for d in distances)
-    z = lax.rem(place[0], depth)
+    z = lax.rem(place[2], depth)
     rows = 2 * depth
     for turn, share_ref in enumerate(share_refs):
         for e in range(2):
@@ -234,10 +244,10 @@
     for query_ref, group in zip(query_refs, distances):
         for at, distance in enumerate(group):
             source = lax.rem(z + depth - distance, depth)
-            for p in range(2):
-                vectors = held[pl.ds(p * depth + source, 2 * planes, stride=rows), :].astype(BF16)
-                part = dot(vectors, query_ref[at, p], NT)
-                total = part if total is None else total + part
+            vectors = [held[pl.ds(p * depth + source, 2 * planes, stride=rows), :] for p in range(2)]
+            wanted = [query_ref[at, p] for p in range(2)]
+            part = dot(jnp.concatenate(vectors, axis=1).astype(BF16), jnp.concatenate(wanted, axis=1), NT)
+            total = part if total is None else total + part
     for turn, out_ref in enumerate(out_refs):
         out_ref[...] = total[2 * turn : 2 * turn + 2, :]
 
@@ -296,7 +306,8 @@
     widen()
     acts = (v_grad, attn_in, out_grad, mlp_hidden)
     weights = (proj_out_value, proj_in_attn, proj_out_mlp, proj_in_mlp)
-    theirs, own = project(jnp.stack([chip, core]).astype(jnp.int32), acts, weights)
+    place = jnp.stack([chip, core, dp_pos, tp_pos]).astype(jnp.int32)
+    theirs, own = project(place, acts, weights)
     theirs, own, queries[1] = lax.optimization_barrier((theirs, own, queries[1]))
     other = lax.ppermute(theirs, "tensor", [(k, k ^ 1) for k in range(width)])
     kept, *sent = add_cores(own, other)
@@ -309,7 +320,6 @@
     partial = outer(parts, rank, width)
     sums = lax.all_to_all(partial, "tensor", 0, 0, tiled=True)
     sums, queries[3] = lax.optimization_barrier((sums, queries[3]))
-    place = jnp.stack([dp_pos, tp_pos]).astype(jnp.int32)
     send, norms, *shares = features(place, sums, 1.0 / math.sqrt(length), dp, planes)
     shares = [shares[0]] + [along_y(shares[turn], turn) for turn in range(1, planes)]
     got = lax.all_to_all(send, "dp", 0, 0, tiled=True)

time: 70.1 us -> 68.7 us (0.980)
  blocking collectives: 0 us -> 10.2 us
  waiting for transfers between devices: 20.2 us -> 14.4 us
  starting transfers between devices: 35.6 us -> 31.5 us
  Pallas kernels: 12.5 us -> 11.1 us
    all_to_all x0 -> x1, blocking collectives: none -> 10.2 us  [shards(): sums = lax.all_to_all(partial, 'tensor', 0, 0, tiled=True)]
    all_to_all x1 -> x0, waiting for transfers between devices: 6.06 us -> none  [shards(): sums = lax.all_to_all(partial, 'tensor', 0, 0, tiled=True)]
    all_to_all x1 -> x0, starting transfers between devices: 4.22 us -> none  [shards(): sums = lax.all_to_all(partial, 'tensor', 0, 0, tiled=True)]
  transfers between devices with their start and end apart: 15 -> 14, of which waited for: 8 -> 7; matrix products, arithmetic and copies ran while one was open for 0% -> 0% of each run, Pallas kernels for 16% -> 14%
where the time goes in v3:
time: 68.7 us; the launch traced here: 68.5 us
  starting transfers between devices  31.5 us (46%)
  waiting for transfers between devices  14.4 us (21%)
  Pallas kernels  11.1 us (16%)
  blocking collectives  10.2 us (15%)
  between operations  0.7 us (1%)
  other arithmetic  0.69 us (1%)
    all_to_all x1, blocking collectives, shards(): sums = lax.all_to_all(partial, 'tensor', 0, 0, tiled=True)  10.2 us
    ppermute x6, starting transfers between devices, along_y(): lax.ppermute(x, 'dp', [(k, (k + turn * depth) % dp) for k in range(dp)])  9.91 us
    ppermute x3, starting transfers between devices, along_z(): lax.ppermute(x, 'dp', [(k, k // depth * depth + (k + turn) % depth) for k...  8.01 us
    all_to_all x1, starting transfers between devices, shards(): got = lax.all_to_all(send, 'dp', 0, 0, tiled=True)  7.11 us
    pallas_call x1, Pallas kernels, project(): pl.pallas_call(project_kernel, out_shape=[pltpu.VMEM((4, half, LANES), F3...  6.82 us
    ppermute x3, starting transfers between devices, shards(): lax.ppermute(sent[s - 1], 'tensor', [(k, (k + 2 * s) % width) for k in ra...  6.35 us
    ppermute x3, waiting for transfers between devices, along_z(): lax.ppermute(x, 'dp', [(k, k // depth * depth + (k + turn) % depth) for k...  5.47 us
    ppermute x6, waiting for transfers between devices, along_y(): lax.ppermute(x, 'dp', [(k, (k + turn * depth) % dp) for k in range(dp)])  4.13 us
  transfers between devices with their start and end apart: 14, of which 7 were waited for; matrix products, arithmetic and copies ran while one was open for 0% of the time, Pallas kernels for 14%

profile of v3, /device:TPU:32, one launch (start us, length us, event | category | flops | bytes accessed | tf_op | source)
XLA Modules:
  0.0 68.5 jit_solution(12044720675019829977)
XLA Ops:
  0.6 6.4 %collective-permute-start = (bf16[1,2,128,128]{3,2,1,0:T(8,128)(2,1)}, bf16[1,2,128,128]{3,2,1,0:T(8,128)(2,1)S(1)}, u32[]{:S(2)}, u32[]{:S(2)}) collective-permute-start(bf16[1,2,128,128]{3,2,1,0:T(8,128)(2,1)} %bitcast.10), channel_id=1, source_target_pairs={{0,32},{8,40},{16,48},{24,56},{32,0},{40,8},{48,16},{56,24},{64,96... | collective-permute-start | bytes 196616 | tf_op jit(solution)/shard_map/ppermute | solution.py:294
  7.0 0.1 pad_add_fusion.place
  7.1 6.8 %project.1 = (f32[4,512,128]{2,1,0:T(8,128)S(1)}, f32[4,512,128]{2,1,0:T(8,128)S(1)}) custom-call(s32[4]{0:T(128)S(1)} %pad_add_fusion.place, bf16[2,1024,128]{2,1,0:T(8,128)(2,1)} %v.1, bf16[2,1024,512]{2,1,0:T(8,128)(2,1)} %a.1, bf16[2,1024,512]{2,1,0:T(8,128)(2,1)} %g.1, bf16[2,1024,1792]{2,1,0:T(8,128)(2,1)} %m.1, bf16[64,128]{1,0:T(8,128)(2,1)} %wv.1, ...), custom_call_target="tpu_custom_call" | custom-call | flops 771751936 | bytes 12058624 | tf_op jit(solution)/shard_map/project/pallas_call | solution.py:79
  13.9 0.0 copy-start
  13.9 0.0 collective-permute-done.refs_1_
  13.9 0.1 collective-permute-start.1
  14.0 2.6 %collective-permute-done.1.other_ref = f32[4,512,128]{2,1,0:T(8,128)S(1)} collective-permute-done((f32[4,512,128]{2,1,0:T(8,128)S(1)}, f32[4,512,128]{2,1,0:T(8,128)S(1)}, u32[]{:S(2)}, u32[]{:S(2)}) %collective-permute-start.1) | collective-permute-done | bytes 1048608 | tf_op jit(solution)/shard_map/ppermute | solution.py:312
  16.7 0.1 add_cores.1
  16.8 3.1 %collective-permute-start.2 = (f32[512,128]{1,0:T(8,128)S(1)}, f32[512,128]{1,0:T(8,128)S(1)}, u32[]{:S(2)}, u32[]{:S(2)}) collective-permute-start(f32[512,128]{1,0:T(8,128)S(1)} %get-tuple-element.32), channel_id=1, source_target_pairs={{0,4},{1,5},{2,6},{3,7},{4,0},{5,1},{6,2},{7,3},{8,12},{9,13},{10,... | collective-permute-start | bytes 786440 | tf_op jit(solution)/shard_map/ppermute | solution.py:316
  19.9 0.0 copy-done
  19.9 1.5 %collective-permute-start.3 = (bf16[2,2,128,128]{3,2,1,0:T(8,128)(2,1)S(1)}, bf16[2,2,128,128]{3,2,1,0:T(8,128)(2,1)S(1)}, u32[]{:S(2)}, u32[]{:S(2)}) collective-permute-start(bf16[2,2,128,128]{3,2,1,0:T(8,128)(2,1)S(1)} %pad_maximum_fusion.1), channel_id=1, source_target_pairs={{0,16},{8,24},{16,32},{24,40},{32,48},{40,56},{48,0},{56,8},{64,80... | collective-permute-start | bytes 393224 | tf_op jit(solution)/shard_map/ppermute | solution.py:294
  21.5 0.6 collective-permute-start.4
  22.1 2.6 %collective-permute-start.5 = (f32[512,128]{1,0:T(8,128)S(1)}, f32[512,128]{1,0:T(8,128)S(1)}, u32[]{:S(2)}, u32[]{:S(2)}) collective-permute-start(f32[512,128]{1,0:T(8,128)S(1)} %get-tuple-element.37), channel_id=1, source_target_pairs={{0,6},{1,7},{2,0},{3,1},{4,2},{5,3},{6,4},{7,5},{8,14},{9,15},{10,... | collective-permute-start | bytes 786440 | tf_op jit(solution)/shard_map/ppermute | solution.py:316
  24.7 5.5 %collective-permute-done.3.refs_2_ = bf16[2,2,128,128]{3,2,1,0:T(8,128)(2,1)S(1)} collective-permute-done((bf16[2,2,128,128]{3,2,1,0:T(8,128)(2,1)S(1)}, bf16[2,2,128,128]{3,2,1,0:T(8,128)(2,1)S(1)}, u32[]{:S(2)}, u32[]{:S(2)}) %collective-permute-start.3) | collective-permute-done | bytes 131104 | tf_op jit(solution)/shard_map/ppermute | solution.py:294
  30.2 0.0 collective-permute-done.2.c_ref
  30.2 0.1 collective-permute-start.6
  30.3 2.0 %collective-permute-done.4.b_ref = f32[512,128]{1,0:T(8,128)S(1)} collective-permute-done((f32[512,128]{1,0:T(8,128)S(1)}, f32[512,128]{1,0:T(8,128)S(1)}, u32[]{:S(2)}, u32[]{:S(2)}) %collective-permute-start.4) | collective-permute-done | bytes 262176 | tf_op jit(solution)/shard_map/ppermute | solution.py:316
  32.3 0.1 collective-permute-done.5.d_ref
  32.4 0.3 outer.1
  32.7 10.2 %all_to_all.10.sums_ref = f32[8,32,128]{2,1,0:T(8,128)S(1)} all-to-all(f32[8,32,128]{2,1,0:T(8,128)S(1)} %outer.1), channel_id=1, replica_groups=mesh['dp'=32,'tensor'=8] {'tensor'}, dimensions={0} | all-to-all | bytes 262144 | tf_op jit(solution)/shard_map/all_to_all | solution.py:321
  42.9 0.0 collective-permute-done.6.refs_3_
  42.9 1.4 %features.1 = (bf16[32,2,16,128]{3,2,1,0:T(8,128)(2,1)}, f32[2,128]{1,0:T(2,128)S(1)}, f32[2,16,128]{2,1,0:T(8,128)S(1)}, f32[2,16,128]{2,1,0:T(8,128)S(1)}, f32...) custom-call(s32[4]{0:T(128)S(1)} %pad_add_fusion.place, f32[8,32,128]{2,1,0:T(8,128)S(1)} %all_to_all.10.sums_ref), custom_call_target="tpu_custom_call" | custom-call | tf_op jit(solution)/shard_map/features/pallas_call | solution.py:182
  44.3 7.1 %all-to-all-start.1 = ((bf16[32,2,16,128]{3,2,1,0:T(8,128)(2,1)}), bf16[32,2,16,128]{3,2,1,0:T(8,128)(2,1)S(1)}, u32[]{:S(2)}, u32[]{:S(2)}) async-start(bf16[32,2,16,128]{3,2,1,0:T(8,128)(2,1)} %get-tuple-element.45), calls=%async_computation.1 | async-start | bytes 524288 | tf_op jit(solution)/shard_map/all_to_all | solution.py:325
  51.4 1.5 %collective-permute-start.7 = (f32[2,16,128]{2,1,0:T(8,128)S(1)}, f32[2,16,128]{2,1,0:T(8,128)S(1)}, u32[]{:S(2)}, u32[]{:S(2)}) collective-permute-start(f32[2,16,128]{2,1,0:T(8,128)S(1)} %get-tuple-element.41), channel_id=1, source_target_pairs={{0,64},{8,72},{16,80},{24,88},{32,96},{40,104},{48,112},{56,120},{... | collective-permute-start | bytes 49160 | tf_op jit(solution)/shard_map/ppermute | solution.py:297
  53.0 2.7 %collective-permute-start.8 = (f32[2,16,128]{2,1,0:T(8,128)S(1)}, f32[2,16,128]{2,1,0:T(8,128)S(1)}, u32[]{:S(2)}, u32[]{:S(2)}) collective-permute-start(f32[2,16,128]{2,1,0:T(8,128)S(1)} %get-tuple-element.42), channel_id=1, source_target_pairs={{0,128},{8,136},{16,144},{24,152},{32,160},{40,168},{48,176},{56,1... | collective-permute-start | bytes 49160 | tf_op jit(solution)/shard_map/ppermute | solution.py:297
  55.7 1.4 %collective-permute-start.9 = (f32[2,16,128]{2,1,0:T(8,128)S(1)}, f32[2,16,128]{2,1,0:T(8,128)S(1)}, u32[]{:S(2)}, u32[]{:S(2)}) collective-permute-start(f32[2,16,128]{2,1,0:T(8,128)S(1)} %get-tuple-element.43), channel_id=1, source_target_pairs={{0,192},{8,200},{16,208},{24,216},{32,224},{40,232},{48,240},{56,2... | collective-permute-start | bytes 49160 | tf_op jit(solution)/shard_map/ppermute | solution.py:297
  57.1 0.0 collective-permute-done.7.refs_5_
  57.1 1.2 %collective-permute-done.8.refs_6_ = f32[2,16,128]{2,1,0:T(8,128)S(1)} collective-permute-done((f32[2,16,128]{2,1,0:T(8,128)S(1)}, f32[2,16,128]{2,1,0:T(8,128)S(1)}, u32[]{:S(2)}, u32[]{:S(2)}) %collective-permute-start.8) | collective-permute-done | bytes 16416 | tf_op jit(solution)/shard_map/ppermute | solution.py:297
  58.3 1.2 %collective-permute-done.9.refs_7_ = f32[2,16,128]{2,1,0:T(8,128)S(1)} collective-permute-done((f32[2,16,128]{2,1,0:T(8,128)S(1)}, f32[2,16,128]{2,1,0:T(8,128)S(1)}, u32[]{:S(2)}, u32[]{:S(2)}) %collective-permute-start.9) | collective-permute-done | bytes 16416 | tf_op jit(solution)/shard_map/ppermute | solution.py:297
  59.4 0.8 %score_shares.1 = (f32[2,128]{1,0:T(2,128)S(1)}, f32[2,128]{1,0:T(2,128)S(1)}, f32[2,128]{1,0:T(2,128)S(1)}, f32[2,128]{1,0:T(2,128)S(1)}) custom-call(s32[4]{0:T(128)S(1)} %pad_add_fusion.place, bf16[1,2,128,128]{3,2,1,0:T(8,128)(2,1)S(1)} %bitcast.13, bf16[1,2,128,128]{3,2,1,0:T(8,128)(2,1)S(1)} %collective-permute-done.refs_1_, ...), custom_call_target="tpu_custom_call" | custom-call | flops 4194304 | bytes 524288 | tf_op jit(solution)/shard_map/score_shares/pallas_call | solution.py:259
  60.2 0.3 collective-permute-start.12
  60.5 3.9 %collective-permute-start.11 = (f32[2,128]{1,0:T(2,128)S(1)}, f32[2,128]{1,0:T(2,128)S(1)}, u32[]{:S(2)}, u32[]{:S(2)}) collective-permute-start(f32[2,128]{1,0:T(2,128)S(1)} %get-tuple-element.49), channel_id=1, source_target_pairs={{0,128},{8,136},{16,144},{24,152},{32,160},{40,168},{48,176},{56,1... | collective-permute-start | bytes 3080 | tf_op jit(solution)/shard_map/ppermute | solution.py:297
  64.3 0.1 collective-permute-start.10
  64.4 0.0 all-to-all-done.1.got_ref
  64.4 1.7 %fisher.1 = f32[1024,128]{1,0:T(8,128)} custom-call(s32[4]{0:T(128)S(1)} %pad_add_fusion.place, bf16[32,2,16,128]{3,2,1,0:T(8,128)(2,1)S(1)} %all-to-all-done.1.got_ref), custom_call_target="tpu_custom_call" | custom-call | tf_op jit(solution)/shard_map/fisher/pallas_call | solution.py:220
  66.1 0.0 collective-permute-done.12
  66.1 0.0 collective-permute-done.11
  66.1 1.8 %collective-permute-done.10 = f32[2,128]{1,0:T(2,128)S(1)} collective-permute-done((f32[2,128]{1,0:T(2,128)S(1)}, f32[2,128]{1,0:T(2,128)S(1)}, u32[]{:S(2)}, u32[]{:S(2)}) %collective-permute-start.10) | collective-permute-done | bytes 1056 | tf_op jit(solution)/shard_map/ppermute | solution.py:297
  67.9 0.6 add_divide_fusion
  (2 shorter events, 0.0 us)
Async XLA Ops:
  0.6 13.3 %collective-permute-start = (bf16[1,2,128,128]{3,2,1,0:T(8,128)(2,1)}, bf16[1,2,128,128]{3,2,1,0:T(8,128)(2,1)S(1)}, u32[]{:S(2)}, u32[]{:S(2)}) collective-permute-start(bf16[1,2,128,128]{3,2,1,0:T(8,128)(2,1)} %bitcast.10), channel_id=1, source_target_pairs={{0,32},{8,40},{16,48},{24,56},{32,0},{40,8},{48,16},{56,24},{64,96... | collective-permute-start | bytes 196616 | tf_op jit(solution)/shard_map/ppermute | solution.py:294
  13.9 6.0 %copy-start = (bf16[2,128,128]{2,1,0:T(8,128)(2,1)S(1)}, bf16[2,128,128]{2,1,0:T(8,128)(2,1)}, u32[]{:S(2)}) copy-start(bf16[2,128,128]{2,1,0:T(8,128)(2,1)} %param.17) | copy-start | bytes 196612
  13.9 2.7 %collective-permute-start.1 = (f32[4,512,128]{2,1,0:T(8,128)S(1)}, f32[4,512,128]{2,1,0:T(8,128)S(1)}, u32[]{:S(2)}, u32[]{:S(2)}) collective-permute-start(f32[4,512,128]{2,1,0:T(8,128)S(1)} %get-tuple-element.31), channel_id=1, source_target_pairs={{0,1},{1,0},{2,3},{3,2},{4,5},{5,4},{6,7},{7,6},{8,9},{9,8},{10,11... | collective-permute-start | bytes 3145736 | tf_op jit(solution)/shard_map/ppermute | solution.py:312
  16.8 13.4 %collective-permute-start.2 = (f32[512,128]{1,0:T(8,128)S(1)}, f32[512,128]{1,0:T(8,128)S(1)}, u32[]{:S(2)}, u32[]{:S(2)}) collective-permute-start(f32[512,128]{1,0:T(8,128)S(1)} %get-tuple-element.32), channel_id=1, source_target_pairs={{0,4},{1,5},{2,6},{3,7},{4,0},{5,1},{6,2},{7,3},{8,12},{9,13},{10,... | collective-permute-start | bytes 786440 | tf_op jit(solution)/shard_map/ppermute | solution.py:316
  19.9 10.3 %collective-permute-start.3 = (bf16[2,2,128,128]{3,2,1,0:T(8,128)(2,1)S(1)}, bf16[2,2,128,128]{3,2,1,0:T(8,128)(2,1)S(1)}, u32[]{:S(2)}, u32[]{:S(2)}) collective-permute-start(bf16[2,2,128,128]{3,2,1,0:T(8,128)(2,1)S(1)} %pad_maximum_fusion.1), channel_id=1, source_target_pairs={{0,16},{8,24},{16,32},{24,40},{32,48},{40,56},{48,0},{56,8},{64,80... | collective-permute-start | bytes 393224 | tf_op jit(solution)/shard_map/ppermute | solution.py:294
  21.5 10.9 %collective-permute-start.4 = (f32[512,128]{1,0:T(8,128)S(1)}, f32[512,128]{1,0:T(8,128)S(1)}, u32[]{:S(2)}, u32[]{:S(2)}) collective-permute-start(f32[512,128]{1,0:T(8,128)S(1)} %get-tuple-element.35), channel_id=1, source_target_pairs={{0,2},{1,3},{2,4},{3,5},{4,6},{5,7},{6,0},{7,1},{8,10},{9,11},{10,... | collective-permute-start | bytes 786440 | tf_op jit(solution)/shard_map/ppermute | solution.py:316
  22.1 10.4 %collective-permute-start.5 = (f32[512,128]{1,0:T(8,128)S(1)}, f32[512,128]{1,0:T(8,128)S(1)}, u32[]{:S(2)}, u32[]{:S(2)}) collective-permute-start(f32[512,128]{1,0:T(8,128)S(1)} %get-tuple-element.37), channel_id=1, source_target_pairs={{0,6},{1,7},{2,0},{3,1},{4,2},{5,3},{6,4},{7,5},{8,14},{9,15},{10,... | collective-permute-start | bytes 786440 | tf_op jit(solution)/shard_map/ppermute | solution.py:316
  30.2 12.7 %collective-permute-start.6 = (bf16[4,2,128,128]{3,2,1,0:T(8,128)(2,1)S(1)}, bf16[4,2,128,128]{3,2,1,0:T(8,128)(2,1)S(1)}, u32[]{:S(2)}, u32[]{:S(2)}) collective-permute-start(bf16[4,2,128,128]{3,2,1,0:T(8,128)(2,1)S(1)} %pad_maximum_fusion), channel_id=1, source_target_pairs={{0,8},{8,16},{16,24},{24,32},{32,40},{40,48},{48,56},{56,0},{64,72... | collective-permute-start | bytes 786440 | tf_op jit(solution)/shard_map/ppermute | solution.py:294
  44.3 20.2 %all-to-all-start.1 = ((bf16[32,2,16,128]{3,2,1,0:T(8,128)(2,1)}), bf16[32,2,16,128]{3,2,1,0:T(8,128)(2,1)S(1)}, u32[]{:S(2)}, u32[]{:S(2)}) async-start(bf16[32,2,16,128]{3,2,1,0:T(8,128)(2,1)} %get-tuple-element.45), calls=%async_computation.1 | async-start | bytes 524288 | tf_op jit(solution)/shard_map/all_to_all | solution.py:325
  51.4 5.7 %collective-permute-start.7 = (f32[2,16,128]{2,1,0:T(8,128)S(1)}, f32[2,16,128]{2,1,0:T(8,128)S(1)}, u32[]{:S(2)}, u32[]{:S(2)}) collective-permute-start(f32[2,16,128]{2,1,0:T(8,128)S(1)} %get-tuple-element.41), channel_id=1, source_target_pairs={{0,64},{8,72},{16,80},{24,88},{32,96},{40,104},{48,112},{56,120},{... | collective-permute-start | bytes 49160 | tf_op jit(solution)/shard_map/ppermute | solution.py:297
  53.0 5.3 %collective-permute-start.8 = (f32[2,16,128]{2,1,0:T(8,128)S(1)}, f32[2,16,128]{2,1,0:T(8,128)S(1)}, u32[]{:S(2)}, u32[]{:S(2)}) collective-permute-start(f32[2,16,128]{2,1,0:T(8,128)S(1)} %get-tuple-element.42), channel_id=1, source_target_pairs={{0,128},{8,136},{16,144},{24,152},{32,160},{40,168},{48,176},{56,1... | collective-permute-start | bytes 49160 | tf_op jit(solution)/shard_map/ppermute | solution.py:297
  55.7 3.8 %collective-permute-start.9 = (f32[2,16,128]{2,1,0:T(8,128)S(1)}, f32[2,16,128]{2,1,0:T(8,128)S(1)}, u32[]{:S(2)}, u32[]{:S(2)}) collective-permute-start(f32[2,16,128]{2,1,0:T(8,128)S(1)} %get-tuple-element.43), channel_id=1, source_target_pairs={{0,192},{8,200},{16,208},{24,216},{32,224},{40,232},{48,240},{56,2... | collective-permute-start | bytes 49160 | tf_op jit(solution)/shard_map/ppermute | solution.py:297
  60.2 5.9 %collective-permute-start.12 = (f32[2,128]{1,0:T(2,128)S(1)}, f32[2,128]{1,0:T(2,128)S(1)}, u32[]{:S(2)}, u32[]{:S(2)}) collective-permute-start(f32[2,128]{1,0:T(2,128)S(1)} %get-tuple-element.50), channel_id=1, source_target_pairs={{0,64},{8,72},{16,80},{24,88},{32,96},{40,104},{48,112},{56,120},{... | collective-permute-start | bytes 3080 | tf_op jit(solution)/shard_map/ppermute | solution.py:297
  60.5 5.6 %collective-permute-start.11 = (f32[2,128]{1,0:T(2,128)S(1)}, f32[2,128]{1,0:T(2,128)S(1)}, u32[]{:S(2)}, u32[]{:S(2)}) collective-permute-start(f32[2,128]{1,0:T(2,128)S(1)} %get-tuple-element.49), channel_id=1, source_target_pairs={{0,128},{8,136},{16,144},{24,152},{32,160},{40,168},{48,176},{56,1... | collective-permute-start | bytes 3080 | tf_op jit(solution)/shard_map/ppermute | solution.py:297
  64.3 3.6 %collective-permute-start.10 = (f32[2,128]{1,0:T(2,128)S(1)}, f32[2,128]{1,0:T(2,128)S(1)}, u32[]{:S(2)}, u32[]{:S(2)}) collective-permute-start(f32[2,128]{1,0:T(2,128)S(1)} %get-tuple-element.48), channel_id=1, source_target_pairs={{0,192},{8,200},{16,208},{24,216},{32,224},{40,232},{48,240},{56,2... | collective-permute-start | bytes 3080 | tf_op jit(solution)/shard_map/ppermute | solution.py:297

commit v4 on v3

--- a/solution.py
+++ b/solution.py
@@ -296,31 +296,28 @@
     def along_y(x, turn):
         return lax.ppermute(x, "dp", [(k, (k + turn * depth) % dp) for k in range(dp)])
 
-    distances, queries = [[0]], [query_features[None]]
-
-    def widen():
-        reach = depth // 2 ** len(queries)
-        queries.append(along_z(jnp.concatenate(queries, axis=0) if len(queries) > 1 else queries[0], reach))
-        distances.append([d + reach for group in distances for d in group])
-
-    widen()
+    own_queries = query_features[None]
+    opposite = along_z(own_queries, depth // 2)
+
     acts = (v_grad, attn_in, out_grad, mlp_hidden)
     weights = (proj_out_value, proj_in_attn, proj_out_mlp, proj_in_mlp)
     place = jnp.stack([chip, core, dp_pos, tp_pos]).astype(jnp.int32)
     theirs, own = project(place, acts, weights)
-    theirs, own, queries[1] = lax.optimization_barrier((theirs, own, queries[1]))
+    theirs, own, opposite = lax.optimization_barrier((theirs, own, opposite))
     other = lax.ppermute(theirs, "tensor", [(k, k ^ 1) for k in range(width)])
     kept, *sent = add_cores(own, other)
-    widen()
+    kept, opposite = lax.optimization_barrier((kept, opposite))
+    pair = jnp.concatenate([own_queries, opposite], axis=0)
+    turns = (0, 1, 2, -1)
+    queries = [along_z(pair, turn) if turn else pair for turn in turns]
+    distances = [[turn % depth, (turn + depth // 2) % depth] for turn in turns]
     parts = [kept] + [
         lax.ppermute(sent[s - 1], "tensor", [(k, (k + 2 * s) % width) for k in range(width)]) for s in (1, 2, 3)
     ]
-    parts[2], queries[2] = lax.optimization_barrier((parts[2], queries[2]))
-    widen()
     partial = outer(parts, rank, width)
     sums = lax.all_to_all(partial, "tensor", 0, 0, tiled=True)
-    sums, queries[3] = lax.optimization_barrier((sums, queries[3]))
     send, norms, *shares = features(place, sums, 1.0 / math.sqrt(length), dp, planes)
+    send, *queries = lax.optimization_barrier((send, *queries))
     shares = [shares[0]] + [along_y(shares[turn], turn) for turn in range(1, planes)]
     got = lax.all_to_all(send, "dp", 0, 0, tiled=True)
     scored = list(score_shares(place, queries, distances, shares))

time: 68.7 us -> 69.4 us (1.010)
  starting transfers between devices: 31.5 us -> 32.4 us
    ppermute x3 -> x4, waiting for transfers between devices: 5.47 us -> 0.01 us  [along_z(): lax.ppermute(x, 'dp', [(k, k // depth * depth + (k + turn) % depth) for k...]
    ppermute x3, waiting for transfers between devices: 2.13 us -> 6.9 us  [shards(): lax.ppermute(sent[s - 1], 'tensor', [(k, (k + 2 * s) % width) for k in ra...]
    ppermute x3 -> x4, starting transfers between devices: 8.01 us -> 9.96 us  [along_z(): lax.ppermute(x, 'dp', [(k, k // depth * depth + (k + turn) % depth) for k...]
    ppermute x6, waiting for transfers between devices: 4.13 us -> 4.83 us  [along_y(): lax.ppermute(x, 'dp', [(k, (k + turn * depth) % dp) for k in range(dp)])]
  transfers between devices with their start and end apart: 14 -> 15, of which waited for: 7 -> 6; matrix products, arithmetic and copies ran while one was open for 0% -> 0% of each run, Pallas kernels for 14% -> 16%
where the time goes in v4:
time: 69.4 us; the launch traced here: 69.1 us
  starting transfers between devices  32.4 us (47%)
  waiting for transfers between devices  14.4 us (21%)
  Pallas kernels  11.1 us (16%)
  blocking collectives  9.87 us (14%)
  between operations  0.7 us (1%)
    ppermute x4, starting transfers between devices, along_z(): lax.ppermute(x, 'dp', [(k, k // depth * depth + (k + turn) % depth) for k...  9.96 us
    all_to_all x1, blocking collectives, shards(): sums = lax.all_to_all(partial, 'tensor', 0, 0, tiled=True)  9.87 us
    ppermute x6, starting transfers between devices, along_y(): lax.ppermute(x, 'dp', [(k, (k + turn * depth) % dp) for k in range(dp)])  9.26 us
    all_to_all x1, starting transfers between devices, shards(): got = lax.all_to_all(send, 'dp', 0, 0, tiled=True)  7.4 us
    ppermute x3, waiting for transfers between devices, shards(): lax.ppermute(sent[s - 1], 'tensor', [(k, (k + 2 * s) % width) for k in ra...  6.9 us
    pallas_call x1, Pallas kernels, project(): pl.pallas_call(project_kernel, out_shape=[pltpu.VMEM((4, half, LANES), F3...  6.82 us
    ppermute x3, starting transfers between devices, shards(): lax.ppermute(sent[s - 1], 'tensor', [(k, (k + 2 * s) % width) for k in ra...  5.73 us
    ppermute x6, waiting for transfers between devices, along_y(): lax.ppermute(x, 'dp', [(k, (k + turn * depth) % dp) for k in range(dp)])  4.83 us
  transfers between devices with their start and end apart: 15, of which 6 were waited for; matrix products, arithmetic and copies ran while one was open for 0% of the time, Pallas kernels for 16%

profile of v4, /device:TPU:32, one launch (start us, length us, event | category | flops | bytes accessed | tf_op | source)
XLA Modules:
  0.0 69.1 jit_solution(13143270238061724334)
XLA Ops:
  0.6 6.4 %collective-permute-start = (bf16[1,2,128,128]{3,2,1,0:T(8,128)(2,1)}, bf16[1,2,128,128]{3,2,1,0:T(8,128)(2,1)S(1)}, u32[]{:S(2)}, u32[]{:S(2)}) collective-permute-start(bf16[1,2,128,128]{3,2,1,0:T(8,128)(2,1)} %bitcast.11), channel_id=1, source_target_pairs={{0,32},{8,40},{16,48},{24,56},{32,0},{40,8},{48,16},{56,24},{64,96... | collective-permute-start | bytes 196616 | tf_op jit(solution)/shard_map/ppermute | solution.py:294
  7.0 0.1 pad_add_fusion.place
  7.1 6.8 %project.1 = (f32[4,512,128]{2,1,0:T(8,128)S(1)}, f32[4,512,128]{2,1,0:T(8,128)S(1)}) custom-call(s32[4]{0:T(128)S(1)} %pad_add_fusion.place, bf16[2,1024,128]{2,1,0:T(8,128)(2,1)} %v.1, bf16[2,1024,512]{2,1,0:T(8,128)(2,1)} %a.1, bf16[2,1024,512]{2,1,0:T(8,128)(2,1)} %g.1, bf16[2,1024,1792]{2,1,0:T(8,128)(2,1)} %m.1, bf16[64,128]{1,0:T(8,128)(2,1)} %wv.1, ...), custom_call_target="tpu_custom_call" | custom-call | flops 771751936 | bytes 12058624 | tf_op jit(solution)/shard_map/project/pallas_call | solution.py:79
  13.9 0.0 copy-start
  13.9 0.0 collective-permute-done
  13.9 0.1 collective-permute-start.1
  14.0 2.6 %collective-permute-done.1.other_ref = f32[4,512,128]{2,1,0:T(8,128)S(1)} collective-permute-done((f32[4,512,128]{2,1,0:T(8,128)S(1)}, f32[4,512,128]{2,1,0:T(8,128)S(1)}, u32[]{:S(2)}, u32[]{:S(2)}) %collective-permute-start.1) | collective-permute-done | bytes 1048608 | tf_op jit(solution)/shard_map/ppermute | solution.py:307
  16.7 0.1 add_cores.1
  16.8 1.6 %collective-permute-start.2 = (f32[512,128]{1,0:T(8,128)S(1)}, f32[512,128]{1,0:T(8,128)S(1)}, u32[]{:S(2)}, u32[]{:S(2)}) collective-permute-start(f32[512,128]{1,0:T(8,128)S(1)} %get-tuple-element.37), channel_id=1, source_target_pairs={{0,2},{1,3},{2,4},{3,5},{4,6},{5,7},{6,0},{7,1},{8,10},{9,11},{10,... | collective-permute-start | bytes 786440 | tf_op jit(solution)/shard_map/ppermute | solution.py:315
  18.4 2.7 %collective-permute-start.3 = (f32[512,128]{1,0:T(8,128)S(1)}, f32[512,128]{1,0:T(8,128)S(1)}, u32[]{:S(2)}, u32[]{:S(2)}) collective-permute-start(f32[512,128]{1,0:T(8,128)S(1)} %get-tuple-element.38), channel_id=1, source_target_pairs={{0,4},{1,5},{2,6},{3,7},{4,0},{5,1},{6,2},{7,3},{8,12},{9,13},{10,... | collective-permute-start | bytes 786440 | tf_op jit(solution)/shard_map/ppermute | solution.py:315
  21.1 1.4 %collective-permute-start.4 = (f32[512,128]{1,0:T(8,128)S(1)}, f32[512,128]{1,0:T(8,128)S(1)}, u32[]{:S(2)}, u32[]{:S(2)}) collective-permute-start(f32[512,128]{1,0:T(8,128)S(1)} %get-tuple-element.39), channel_id=1, source_target_pairs={{0,6},{1,7},{2,0},{3,1},{4,2},{5,3},{6,4},{7,5},{8,14},{9,15},{10,... | collective-permute-start | bytes 786440 | tf_op jit(solution)/shard_map/ppermute | solution.py:315
  22.5 0.0 copy-done
  22.5 1.1 %collective-permute-start.7 = (bf16[2,2,128,128]{3,2,1,0:T(8,128)(2,1)S(1)}, bf16[2,2,128,128]{3,2,1,0:T(8,128)(2,1)S(1)}, u32[]{:S(2)}, u32[]{:S(2)}) collective-permute-start(bf16[2,2,128,128]{3,2,1,0:T(8,128)(2,1)S(1)} %pad_maximum_fusion.refs_0_), channel_id=1, source_target_pairs={{0,56},{8,0},{16,8},{24,16},{32,24},{40,32},{48,40},{56,48},{64,12... | collective-permute-start | bytes 393224 | tf_op jit(solution)/shard_map/ppermute | solution.py:294
  23.6 1.5 %collective-permute-start.6 = (bf16[2,2,128,128]{3,2,1,0:T(8,128)(2,1)S(1)}, bf16[2,2,128,128]{3,2,1,0:T(8,128)(2,1)S(1)}, u32[]{:S(2)}, u32[]{:S(2)}) collective-permute-start(bf16[2,2,128,128]{3,2,1,0:T(8,128)(2,1)S(1)} %pad_maximum_fusion.refs_0_), channel_id=1, source_target_pairs={{0,16},{8,24},{16,32},{24,40},{32,48},{40,56},{48,0},{56,8},{64,80... | collective-permute-start | bytes 393224 | tf_op jit(solution)/shard_map/ppermute | solution.py:294
  25.1 1.3 %collective-permute-done.2.b_ref = f32[512,128]{1,0:T(8,128)S(1)} collective-permute-done((f32[512,128]{1,0:T(8,128)S(1)}, f32[512,128]{1,0:T(8,128)S(1)}, u32[]{:S(2)}, u32[]{:S(2)}) %collective-permute-start.2) | collective-permute-done | bytes 262176 | tf_op jit(solution)/shard_map/ppermute | solution.py:315
  26.4 1.0 %collective-permute-start.5 = (bf16[2,2,128,128]{3,2,1,0:T(8,128)(2,1)S(1)}, bf16[2,2,128,128]{3,2,1,0:T(8,128)(2,1)S(1)}, u32[]{:S(2)}, u32[]{:S(2)}) collective-permute-start(bf16[2,2,128,128]{3,2,1,0:T(8,128)(2,1)S(1)} %pad_maximum_fusion.refs_0_), channel_id=1, source_target_pairs={{0,8},{8,16},{16,24},{24,32},{32,40},{40,48},{48,56},{56,0},{64,72... | collective-permute-start | bytes 393224 | tf_op jit(solution)/shard_map/ppermute | solution.py:294
  27.4 5.6 %collective-permute-done.3.c_ref = f32[512,128]{1,0:T(8,128)S(1)} collective-permute-done((f32[512,128]{1,0:T(8,128)S(1)}, f32[512,128]{1,0:T(8,128)S(1)}, u32[]{:S(2)}, u32[]{:S(2)}) %collective-permute-start.3) | collective-permute-done | bytes 262176 | tf_op jit(solution)/shard_map/ppermute | solution.py:315
  33.0 0.0 collective-permute-done.4.d_ref
  33.0 0.3 outer.1
  33.3 9.9 %all_to_all.10.sums_ref = f32[8,32,128]{2,1,0:T(8,128)S(1)} all-to-all(f32[8,32,128]{2,1,0:T(8,128)S(1)} %outer.1), channel_id=1, replica_groups=mesh['dp'=32,'tensor'=8] {'tensor'}, dimensions={0} | all-to-all | bytes 262144 | tf_op jit(solution)/shard_map/all_to_all | solution.py:318
  43.2 1.4 %features.1 = (bf16[32,2,16,128]{3,2,1,0:T(8,128)(2,1)}, f32[2,128]{1,0:T(2,128)S(1)}, f32[2,16,128]{2,1,0:T(8,128)S(1)}, f32[2,16,128]{2,1,0:T(8,128)S(1)}, f32...) custom-call(s32[4]{0:T(128)S(1)} %pad_add_fusion.place, f32[8,32,128]{2,1,0:T(8,128)S(1)} %all_to_all.10.sums_ref), custom_call_target="tpu_custom_call" | custom-call | tf_op jit(solution)/shard_map/features/pallas_call | solution.py:182
  44.6 0.0 collective-permute-done.7.refs_3_
  44.6 0.0 collective-permute-done.6.refs_2_
  44.6 0.0 collective-permute-done.5.refs_1_
  44.6 7.4 %all-to-all-start.1 = ((bf16[32,2,16,128]{3,2,1,0:T(8,128)(2,1)}), bf16[32,2,16,128]{3,2,1,0:T(8,128)(2,1)S(1)}, u32[]{:S(2)}, u32[]{:S(2)}) async-start(bf16[32,2,16,128]{3,2,1,0:T(8,128)(2,1)} %get-tuple-element.51), calls=%async_computation.1 | async-start | bytes 524288 | tf_op jit(solution)/shard_map/all_to_all | solution.py:322
  52.0 1.5 %collective-permute-start.8 = (f32[2,16,128]{2,1,0:T(8,128)S(1)}, f32[2,16,128]{2,1,0:T(8,128)S(1)}, u32[]{:S(2)}, u32[]{:S(2)}) collective-permute-start(f32[2,16,128]{2,1,0:T(8,128)S(1)} %get-tuple-element.47), channel_id=1, source_target_pairs={{0,64},{8,72},{16,80},{24,88},{32,96},{40,104},{48,112},{56,120},{... | collective-permute-start | bytes 49160 | tf_op jit(solution)/shard_map/ppermute | solution.py:297
  53.6 2.7 %collective-permute-start.9 = (f32[2,16,128]{2,1,0:T(8,128)S(1)}, f32[2,16,128]{2,1,0:T(8,128)S(1)}, u32[]{:S(2)}, u32[]{:S(2)}) collective-permute-start(f32[2,16,128]{2,1,0:T(8,128)S(1)} %get-tuple-element.48), channel_id=1, source_target_pairs={{0,128},{8,136},{16,144},{24,152},{32,160},{40,168},{48,176},{56,1... | collective-permute-start | bytes 49160 | tf_op jit(solution)/shard_map/ppermute | solution.py:297
  56.3 1.4 %collective-permute-start.10 = (f32[2,16,128]{2,1,0:T(8,128)S(1)}, f32[2,16,128]{2,1,0:T(8,128)S(1)}, u32[]{:S(2)}, u32[]{:S(2)}) collective-permute-start(f32[2,16,128]{2,1,0:T(8,128)S(1)} %get-tuple-element.49), channel_id=1, source_target_pairs={{0,192},{8,200},{16,208},{24,216},{32,224},{40,232},{48,240},{56,2... | collective-permute-start | bytes 49160 | tf_op jit(solution)/shard_map/ppermute | solution.py:297
  57.7 0.0 collective-permute-done.8.refs_5_
  57.7 1.2 %collective-permute-done.9.refs_6_ = f32[2,16,128]{2,1,0:T(8,128)S(1)} collective-permute-done((f32[2,16,128]{2,1,0:T(8,128)S(1)}, f32[2,16,128]{2,1,0:T(8,128)S(1)}, u32[]{:S(2)}, u32[]{:S(2)}) %collective-permute-start.9) | collective-permute-done | bytes 16416 | tf_op jit(solution)/shard_map/ppermute | solution.py:297
  58.9 1.2 %collective-permute-done.10.refs_7_ = f32[2,16,128]{2,1,0:T(8,128)S(1)} collective-permute-done((f32[2,16,128]{2,1,0:T(8,128)S(1)}, f32[2,16,128]{2,1,0:T(8,128)S(1)}, u32[]{:S(2)}, u32[]{:S(2)}) %collective-permute-start.10) | collective-permute-done | bytes 16416 | tf_op jit(solution)/shard_map/ppermute | solution.py:297
  60.0 0.8 %score_shares.1 = (f32[2,128]{1,0:T(2,128)S(1)}, f32[2,128]{1,0:T(2,128)S(1)}, f32[2,128]{1,0:T(2,128)S(1)}, f32[2,128]{1,0:T(2,128)S(1)}) custom-call(s32[4]{0:T(128)S(1)} %pad_add_fusion.place, bf16[2,2,128,128]{3,2,1,0:T(8,128)(2,1)S(1)} %pad_maximum_fusion.refs_0_, bf16[2,2,128,128]{3,2,1,0:T(8,128)(2,1)S(1)} %collective-permute-done.5.refs_1_, ...), custom_call_target="tpu_custom_call" | custom-call | flops 4194304 | bytes 524288 | tf_op jit(solution)/shard_map/score_shares/pallas_call | solution.py:259
  60.8 2.7 %collective-permute-start.11 = (f32[2,128]{1,0:T(2,128)S(1)}, f32[2,128]{1,0:T(2,128)S(1)}, u32[]{:S(2)}, u32[]{:S(2)}) collective-permute-start(f32[2,128]{1,0:T(2,128)S(1)} %get-tuple-element.54), channel_id=1, source_target_pairs={{0,192},{8,200},{16,208},{24,216},{32,224},{40,232},{48,240},{56,2... | collective-permute-start | bytes 3080 | tf_op jit(solution)/shard_map/ppermute | solution.py:297
  63.5 0.0 collective-permute-start.12
  63.5 0.9 %collective-permute-start.13 = (f32[2,128]{1,0:T(2,128)S(1)}, f32[2,128]{1,0:T(2,128)S(1)}, u32[]{:S(2)}, u32[]{:S(2)}) collective-permute-start(f32[2,128]{1,0:T(2,128)S(1)} %get-tuple-element.56), channel_id=1, source_target_pairs={{0,64},{8,72},{16,80},{24,88},{32,96},{40,104},{48,112},{56,120},{... | collective-permute-start | bytes 3080 | tf_op jit(solution)/shard_map/ppermute | solution.py:297
  64.4 0.0 all-to-all-done.1.got_ref
  64.4 1.7 %fisher.1 = f32[1024,128]{1,0:T(8,128)} custom-call(s32[4]{0:T(128)S(1)} %pad_add_fusion.place, bf16[32,2,16,128]{3,2,1,0:T(8,128)(2,1)S(1)} %all-to-all-done.1.got_ref), custom_call_target="tpu_custom_call" | custom-call | tf_op jit(solution)/shard_map/fisher/pallas_call | solution.py:220
  66.1 0.0 collective-permute-done.11
  66.1 2.5 %collective-permute-done.12 = f32[2,128]{1,0:T(2,128)S(1)} collective-permute-done((f32[2,128]{1,0:T(2,128)S(1)}, f32[2,128]{1,0:T(2,128)S(1)}, u32[]{:S(2)}, u32[]{:S(2)}) %collective-permute-start.12) | collective-permute-done | bytes 1056 | tf_op jit(solution)/shard_map/ppermute | solution.py:297
  68.6 0.0 collective-permute-done.13
  68.6 0.6 add_divide_fusion
  (1 shorter events, 0.0 us)
Async XLA Ops:
  0.6 13.3 %collective-permute-start = (bf16[1,2,128,128]{3,2,1,0:T(8,128)(2,1)}, bf16[1,2,128,128]{3,2,1,0:T(8,128)(2,1)S(1)}, u32[]{:S(2)}, u32[]{:S(2)}) collective-permute-start(bf16[1,2,128,128]{3,2,1,0:T(8,128)(2,1)} %bitcast.11), channel_id=1, source_target_pairs={{0,32},{8,40},{16,48},{24,56},{32,0},{40,8},{48,16},{56,24},{64,96... | collective-permute-start | bytes 196616 | tf_op jit(solution)/shard_map/ppermute | solution.py:294
  13.9 8.6 %copy-start = (bf16[2,128,128]{2,1,0:T(8,128)(2,1)S(1)}, bf16[2,128,128]{2,1,0:T(8,128)(2,1)}, u32[]{:S(2)}) copy-start(bf16[2,128,128]{2,1,0:T(8,128)(2,1)} %param.17) | copy-start | bytes 196612
  13.9 2.7 %collective-permute-start.1 = (f32[4,512,128]{2,1,0:T(8,128)S(1)}, f32[4,512,128]{2,1,0:T(8,128)S(1)}, u32[]{:S(2)}, u32[]{:S(2)}) collective-permute-start(f32[4,512,128]{2,1,0:T(8,128)S(1)} %get-tuple-element.33), channel_id=1, source_target_pairs={{0,1},{1,0},{2,3},{3,2},{4,5},{5,4},{6,7},{7,6},{8,9},{9,8},{10,11... | collective-permute-start | bytes 3145736 | tf_op jit(solution)/shard_map/ppermute | solution.py:307
  16.8 9.6 %collective-permute-start.2 = (f32[512,128]{1,0:T(8,128)S(1)}, f32[512,128]{1,0:T(8,128)S(1)}, u32[]{:S(2)}, u32[]{:S(2)}) collective-permute-start(f32[512,128]{1,0:T(8,128)S(1)} %get-tuple-element.37), channel_id=1, source_target_pairs={{0,2},{1,3},{2,4},{3,5},{4,6},{5,7},{6,0},{7,1},{8,10},{9,11},{10,... | collective-permute-start | bytes 786440 | tf_op jit(solution)/shard_map/ppermute | solution.py:315
  18.4 14.7 %collective-permute-start.3 = (f32[512,128]{1,0:T(8,128)S(1)}, f32[512,128]{1,0:T(8,128)S(1)}, u32[]{:S(2)}, u32[]{:S(2)}) collective-permute-start(f32[512,128]{1,0:T(8,128)S(1)} %get-tuple-element.38), channel_id=1, source_target_pairs={{0,4},{1,5},{2,6},{3,7},{4,0},{5,1},{6,2},{7,3},{8,12},{9,13},{10,... | collective-permute-start | bytes 786440 | tf_op jit(solution)/shard_map/ppermute | solution.py:315
  21.1 11.9 %collective-permute-start.4 = (f32[512,128]{1,0:T(8,128)S(1)}, f32[512,128]{1,0:T(8,128)S(1)}, u32[]{:S(2)}, u32[]{:S(2)}) collective-permute-start(f32[512,128]{1,0:T(8,128)S(1)} %get-tuple-element.39), channel_id=1, source_target_pairs={{0,6},{1,7},{2,0},{3,1},{4,2},{5,3},{6,4},{7,5},{8,14},{9,15},{10,... | collective-permute-start | bytes 786440 | tf_op jit(solution)/shard_map/ppermute | solution.py:315
  22.5 22.1 %collective-permute-start.7 = (bf16[2,2,128,128]{3,2,1,0:T(8,128)(2,1)S(1)}, bf16[2,2,128,128]{3,2,1,0:T(8,128)(2,1)S(1)}, u32[]{:S(2)}, u32[]{:S(2)}) collective-permute-start(bf16[2,2,128,128]{3,2,1,0:T(8,128)(2,1)S(1)} %pad_maximum_fusion.refs_0_), channel_id=1, source_target_pairs={{0,56},{8,0},{16,8},{24,16},{32,24},{40,32},{48,40},{56,48},{64,12... | collective-permute-start | bytes 393224 | tf_op jit(solution)/shard_map/ppermute | solution.py:294
  23.6 21.0 %collective-permute-start.6 = (bf16[2,2,128,128]{3,2,1,0:T(8,128)(2,1)S(1)}, bf16[2,2,128,128]{3,2,1,0:T(8,128)(2,1)S(1)}, u32[]{:S(2)}, u32[]{:S(2)}) collective-permute-start(bf16[2,2,128,128]{3,2,1,0:T(8,128)(2,1)S(1)} %pad_maximum_fusion.refs_0_), channel_id=1, source_target_pairs={{0,16},{8,24},{16,32},{24,40},{32,48},{40,56},{48,0},{56,8},{64,80... | collective-permute-start | bytes 393224 | tf_op jit(solution)/shard_map/ppermute | solution.py:294
  26.4 18.2 %collective-permute-start.5 = (bf16[2,2,128,128]{3,2,1,0:T(8,128)(2,1)S(1)}, bf16[2,2,128,128]{3,2,1,0:T(8,128)(2,1)S(1)}, u32[]{:S(2)}, u32[]{:S(2)}) collective-permute-start(bf16[2,2,128,128]{3,2,1,0:T(8,128)(2,1)S(1)} %pad_maximum_fusion.refs_0_), channel_id=1, source_target_pairs={{0,8},{8,16},{16,24},{24,32},{32,40},{40,48},{48,56},{56,0},{64,72... | collective-permute-start | bytes 393224 | tf_op jit(solution)/shard_map/ppermute | solution.py:294
  44.6 19.8 %all-to-all-start.1 = ((bf16[32,2,16,128]{3,2,1,0:T(8,128)(2,1)}), bf16[32,2,16,128]{3,2,1,0:T(8,128)(2,1)S(1)}, u32[]{:S(2)}, u32[]{:S(2)}) async-start(bf16[32,2,16,128]{3,2,1,0:T(8,128)(2,1)} %get-tuple-element.51), calls=%async_computation.1 | async-start | bytes 524288 | tf_op jit(solution)/shard_map/all_to_all | solution.py:322
  52.0 5.7 %collective-permute-start.8 = (f32[2,16,128]{2,1,0:T(8,128)S(1)}, f32[2,16,128]{2,1,0:T(8,128)S(1)}, u32[]{:S(2)}, u32[]{:S(2)}) collective-permute-start(f32[2,16,128]{2,1,0:T(8,128)S(1)} %get-tuple-element.47), channel_id=1, source_target_pairs={{0,64},{8,72},{16,80},{24,88},{32,96},{40,104},{48,112},{56,120},{... | collective-permute-start | bytes 49160 | tf_op jit(solution)/shard_map/ppermute | solution.py:297
  53.6 5.3 %collective-permute-start.9 = (f32[2,16,128]{2,1,0:T(8,128)S(1)}, f32[2,16,128]{2,1,0:T(8,128)S(1)}, u32[]{:S(2)}, u32[]{:S(2)}) collective-permute-start(f32[2,16,128]{2,1,0:T(8,128)S(1)} %get-tuple-element.48), channel_id=1, source_target_pairs={{0,128},{8,136},{16,144},{24,152},{32,160},{40,168},{48,176},{56,1... | collective-permute-start | bytes 49160 | tf_op jit(solution)/shard_map/ppermute | solution.py:297
  56.3 3.8 %collective-permute-start.10 = (f32[2,16,128]{2,1,0:T(8,128)S(1)}, f32[2,16,128]{2,1,0:T(8,128)S(1)}, u32[]{:S(2)}, u32[]{:S(2)}) collective-permute-start(f32[2,16,128]{2,1,0:T(8,128)S(1)} %get-tuple-element.49), channel_id=1, source_target_pairs={{0,192},{8,200},{16,208},{24,216},{32,224},{40,232},{48,240},{56,2... | collective-permute-start | bytes 49160 | tf_op jit(solution)/shard_map/ppermute | solution.py:297
  60.8 5.2 %collective-permute-start.11 = (f32[2,128]{1,0:T(2,128)S(1)}, f32[2,128]{1,0:T(2,128)S(1)}, u32[]{:S(2)}, u32[]{:S(2)}) collective-permute-start(f32[2,128]{1,0:T(2,128)S(1)} %get-tuple-element.54), channel_id=1, source_target_pairs={{0,192},{8,200},{16,208},{24,216},{32,224},{40,232},{48,240},{56,2... | collective-permute-start | bytes 3080 | tf_op jit(solution)/shard_map/ppermute | solution.py:297
  63.5 5.1 %collective-permute-start.12 = (f32[2,128]{1,0:T(2,128)S(1)}, f32[2,128]{1,0:T(2,128)S(1)}, u32[]{:S(2)}, u32[]{:S(2)}) collective-permute-start(f32[2,128]{1,0:T(2,128)S(1)} %get-tuple-element.55), channel_id=1, source_target_pairs={{0,128},{8,136},{16,144},{24,152},{32,160},{40,168},{48,176},{56,1... | collective-permute-start | bytes 3080 | tf_op jit(solution)/shard_map/ppermute | solution.py:297
  63.5 5.1 %collective-permute-start.13 = (f32[2,128]{1,0:T(2,128)S(1)}, f32[2,128]{1,0:T(2,128)S(1)}, u32[]{:S(2)}, u32[]{:S(2)}) collective-permute-start(f32[2,128]{1,0:T(2,128)S(1)} %get-tuple-element.56), channel_id=1, source_target_pairs={{0,64},{8,72},{16,80},{24,88},{32,96},{40,104},{48,112},{56,120},{... | collective-permute-start | bytes 3080 | tf_op jit(solution)/shard_map/ppermute | solution.py:297
